TPU v7x, 256 devices: a whole 4x4x8 slice. The times are simulated.
256 devices in a mesh: grp: 2 (over core), seq: 32 (over x, z_lo, y), head: 4 (over z_hi).
Axes of the slice: x: 4, y: 4, z: 8 (z_hi: 4, z_lo: 2; z = z_hi * 2 + z_lo), core: 2. Of those that a mesh axis runs over, the one named last changes fastest.
Arguments:
- queries: bfloat16 [1024, 2048], P(('grp', 'seq'), 'head'), may hold values from -100 to 100
- keys: bfloat16 [2, 32768, 2048], P(None, ('grp', 'seq'), 'head'), may hold values from -15 to 15
- values: bfloat16 [2, 32768, 2048], P(None, ('grp', 'seq'), 'head'), may hold values from -6 to 6
- grad_out: bfloat16 [1024, 2048], P(('grp', 'seq', 'head')), may hold values from -6 to 6
- pad_counts: int32 [2], replicated, may hold values from 0 to 256, as said below
Outputs:
- context: bfloat16 [1024, 2048], P(('grp', 'seq', 'head'))
- grad_queries: bfloat16 [1024, 2048], P(('grp', 'seq'), 'head')
- grad_keys: bfloat16 [2, 32768, 2048], P(None, ('grp', 'seq'), 'head')
- grad_values: bfloat16 [2, 32768, 2048], P(None, ('grp', 'seq'), 'head')
Inputs may be any that keep to these rules, and one draw needn't show every extreme that they name: `pad_counts`: each count is at most 256, and in every draw one pair has exactly 256 padding tokens.
All inputs are finite; a program needn't handle non-finite values.
Results may differ from a plain program's by a relative error of at most 0.0215.
Values may be sent and summed in bfloat16 or wider, within the bound.
A program may use at most 64 MiB of HBM per device.

v0:
```python
import math

import jax
import jax.numpy as jnp
from jax import lax
from jax.sharding import PartitionSpec as P

HEAD_DIM = 64


def valid_rows(pad_counts, first, rows, seq_len):
    position = first + jnp.arange(rows, dtype=jnp.int32)
    which = position // seq_len
    within = position % seq_len
    onehot = which[:, None] == jnp.arange(pad_counts.shape[0], dtype=jnp.int32)[None, :]
    pads = jnp.sum(jnp.where(onehot, pad_counts[None, :], 0), axis=1)
    return (within < seq_len - pads).astype(jnp.float32)


def source_blocks(array, heads_here):
    batch, rows, width = array.shape
    block = math.gcd(rows, 128)
    return array.reshape(batch, rows // block, block, heads_here, HEAD_DIM).transpose(1, 0, 2, 3, 4)


def pair_scores(query_heads, key_block, scale):
    return (
        jnp.einsum("bthd,bphd->bhtp", query_heads, key_block, preferred_element_type=jnp.float32)
        * scale
    )


def local(queries, keys, values, grad_out, pad_counts):
    rows, width = queries.shape
    heads_here = width // HEAD_DIM
    batch = keys.shape[0]
    scale = 1.0 / math.sqrt(HEAD_DIM)
    group = lax.axis_size(("grp", "seq"))
    seq_len = rows * group // batch
    first = lax.axis_index(("grp", "seq")) * rows
    valid = valid_rows(pad_counts, first, rows, seq_len)
    grad_cols = lax.all_to_all(grad_out, "head", split_axis=1, concat_axis=0, tiled=True)
    masked_mine = jnp.where(valid[:, None] > 0, grad_cols, jnp.zeros((), jnp.bfloat16))
    query_all, grad_all = (
        lax.all_gather(queries, ("grp", "seq"), axis=0, tiled=True),
        lax.all_gather(masked_mine, ("grp", "seq"), axis=0, tiled=True),
    )
    query_heads = query_all.reshape(batch, seq_len, heads_here, HEAD_DIM)
    grad_heads = grad_all.reshape(batch, seq_len, heads_here, HEAD_DIM)
    key_blocks = source_blocks(keys, heads_here)
    value_blocks = source_blocks(values, heads_here)

    def stats_step(state, key_block):
        top, total = state
        scores = pair_scores(query_heads, key_block, scale)
        new_top = jnp.maximum(top, jnp.max(scores, axis=-1))
        total = total * jnp.exp(top - new_top) + jnp.sum(
            jnp.exp(scores - new_top[..., None]), axis=-1
        )
        return ((new_top, total), None)

    start = (
        jnp.full((batch, heads_here, seq_len), -1e30, jnp.float32),
        jnp.zeros((batch, heads_here, seq_len), jnp.float32),
    )
    (top, total), unused = lax.scan(stats_step, start, key_blocks)
    row_top = lax.pmax(top, ("grp", "seq"))
    row_total = lax.psum(total * jnp.exp(top - row_top), ("grp", "seq"))

    def forward_step(accum, item):
        key_block, value_block = item
        scores = pair_scores(query_heads, key_block, scale)
        probs = jnp.exp(scores - row_top[..., None]) / row_total[..., None]
        added = jnp.einsum(
            "bhtp,bphd->bthd",
            probs.astype(jnp.bfloat16),
            value_block,
            preferred_element_type=jnp.float32,
        )
        return (accum + added, None)

    partial_value, unused = lax.scan(
        forward_step,
        jnp.zeros((batch, seq_len, heads_here, HEAD_DIM), jnp.float32),
        (key_blocks, value_blocks),
    )
    partial_value = partial_value.reshape(batch * seq_len, width)
    summed = lax.psum(partial_value, ("grp", "seq"))
    attended = lax.dynamic_slice_in_dim(summed, first, rows, 0) * valid[:, None]
    delta_rows = jnp.sum(
        (grad_all.astype(jnp.float32) * summed).reshape(batch * seq_len, heads_here, HEAD_DIM),
        axis=-1,
    )
    delta = delta_rows.reshape(batch, seq_len, heads_here).transpose(0, 2, 1)
    context = lax.all_to_all(
        attended.astype(jnp.bfloat16), "head", split_axis=0, concat_axis=1, tiled=True
    )

    def backward_step(grad_q, item):
        key_block, value_block = item
        scores = pair_scores(query_heads, key_block, scale)
        probs = jnp.exp(scores - row_top[..., None]) / row_total[..., None]
        weights = probs.astype(jnp.bfloat16)
        grad_probs = jnp.einsum(
            "bthd,bphd->bhtp", grad_heads, value_block, preferred_element_type=jnp.float32
        )
        grad_scores = (probs * (grad_probs - delta[..., None]) * scale).astype(jnp.bfloat16)
        grad_q = grad_q + jnp.einsum(
            "bhtp,bphd->bthd", grad_scores, key_block, preferred_element_type=jnp.float32
        )
        grad_k = jnp.einsum(
            "bhtp,bthd->bphd", grad_scores, query_heads, preferred_element_type=jnp.float32
        )
        grad_v = jnp.einsum(
            "bhtp,bthd->bphd", weights, grad_heads, preferred_element_type=jnp.float32
        )
        return (grad_q, (grad_k.astype(jnp.bfloat16), grad_v.astype(jnp.bfloat16)))

    grad_q, (key_parts, value_parts) = lax.scan(
        backward_step,
        jnp.zeros((batch, seq_len, heads_here, HEAD_DIM), jnp.float32),
        (key_blocks, value_blocks),
    )
    src_rows = keys.shape[1]
    grad_keys = key_parts.transpose(1, 0, 2, 3, 4).reshape(batch, src_rows, width)
    grad_values = value_parts.transpose(1, 0, 2, 3, 4).reshape(batch, src_rows, width)
    grad_queries = lax.psum_scatter(
        grad_q.reshape(batch * seq_len, width), ("grp", "seq"), scatter_dimension=0, tiled=True
    )
    return (context, grad_queries.astype(jnp.bfloat16), grad_keys, grad_values)


def solution(mesh):
    return jax.shard_map(
        local,
        mesh=mesh,
        in_specs=(
            P(("grp", "seq"), "head"),
            P(None, ("grp", "seq"), "head"),
            P(None, ("grp", "seq"), "head"),
            P(("grp", "seq", "head"), None),
            P(),
        ),
        out_specs=(
            P(("grp", "seq", "head"), None),
            P(("grp", "seq"), "head"),
            P(None, ("grp", "seq"), "head"),
            P(None, ("grp", "seq"), "head"),
        ),
        check_vma=False,
    )
```

profile of v0, /device:TPU:1, one launch (start us, length us, event | category | flops | bytes accessed | tf_op | source)
XLA Modules:
  0.0 1626.8 jit_solution(12014491093893612905)
XLA Ops:
  7.9 9.0 all-to-all-start.1
  16.9 0.7 fusion.39
  17.7 1.5 copy.83
  19.8 1.5 copy.82
  21.8 1.7 all-to-all-done.1
  24.3 93.7 %all-gather.3.cloned.1.call-done = bf16[1024,512]{1,0:T(8,128)(2,1)} async-done(((bf16[16,512]{1,0:T(8,128)(2,1)}), bf16[1024,512]{1,0:T(8,128)(2,1)}) %all-gather.3.cloned.1.call-update) | async-done | bytes 1048592 | tf_op jit(solution)/shard_map/all_gather | solution.py:45
  118.0 3.9 reshape.110
  121.9 2.5 copy.89
  124.5 6.5 while.39
  124.5 0.8 bitcast_reduce_fusion.3
  125.3 0.8 fusion.67
  126.1 0.8 bitcast_reduce_fusion.3
  126.9 0.8 fusion.67
  127.7 0.8 bitcast_reduce_fusion.3
  128.5 0.8 fusion.67
  129.3 0.8 bitcast_reduce_fusion.3
  130.1 0.8 fusion.67
  130.9 277.8 %pmax.7 = f32[2,8,512]{2,1,0:T(8,128)S(1)} all-reduce(f32[2,8,512]{2,1,0:T(8,128)S(1)} %get-tuple-element.128), channel_id=1, replica_groups=mesh['grp'=2,'seq'=32,'head'=4] {'grp','seq'}, use_global_device_ids=true, to_apply=%region_4.5 | all-reduce | flops 8192 | bytes 65536 | tf_op jit(solution)/shard_map/pmax | solution.py:67
  408.8 275.0 %psum.14 = f32[2,8,512]{2,1,0:T(8,128)S(1)} all-reduce(f32[2,8,512]{2,1,0:T(8,128)S(1)} %exponential_multiply_fusion), channel_id=1, replica_groups=mesh['grp'=2,'seq'=32,'head'=4] {'grp','seq'}, use_global_device_ids=true, to_apply=%region_5.6 | all-reduce | flops 8192 | bytes 65536 | tf_op jit(solution)/shard_map/psum | solution.py:68
  683.8 15.4 while.40
  683.8 2.7 bitcast_add_fusion.4
  686.4 4.3 bitcast_add_fusion.4
  690.7 4.3 bitcast_add_fusion.4
  694.9 4.3 bitcast_add_fusion.4
  699.2 4.2 copy.105
  703.4 4.8 reshape.104
  708.5 3.9 reshape.105
  712.4 2.5 copy.98
  714.9 555.2 %all-reduce.2.cloned.1.call-done = f32[1024,512]{1,0:T(8,128)} async-done(((f32[1024,512]{1,0:T(8,128)}), f32[1024,512]{1,0:T(8,128)}) %all-reduce.2.cloned.1.call-update) | async-done | bytes 2097168 | tf_op jit(solution)/shard_map/psum | solution.py:88
  1270.1 3.5 convert_multiply_fusion
  1273.6 2.9 copy.94
  1276.5 1.8 bitcast_reduce_fusion.1
  1278.3 32.0 %while.41 = (s32[]{:T(128)}, f32[2,512,8,64]{1,3,2,0:T(8,128)}, bf16[4,2,128,8,64]{2,4,3,1,0:T(8,128)(2,1)}, bf16[4,2,128,8,64]{2,4,3,1,0:T(8,128)(2,1)}, bf16[4...) while((s32[]{:T(128)}, f32[2,512,8,64]{1,3,2,0:T(8,128)}, ...), condition=%wide.region_12.13_spmd.clone, body=%wide.region_11.12_spmd.clone.sunk | while | flops 680787968 | bytes 45449432 | solution.py:119
  1278.3 1.0 exponential_divide_fusion.2
  1279.3 1.6 fusion.83
  1280.9 1.8 multiply_convert_fusion.3
  1282.7 1.6 fusion.82
  1285.0 1.3 copy-done.1
  1286.3 1.0 exponential_divide_fusion.2
  1287.3 1.6 fusion.83
  1288.9 1.8 multiply_convert_fusion.3
  1290.7 1.6 fusion.82
  1293.0 1.3 copy-done.1
  1294.3 1.0 exponential_divide_fusion.2
  1295.4 1.6 fusion.83
  1296.9 1.8 multiply_convert_fusion.3
  1298.7 1.6 fusion.82
  1301.0 1.3 copy-done.1
  1302.3 1.0 exponential_divide_fusion.2
  1303.4 1.6 fusion.83
  1304.9 1.8 multiply_convert_fusion.3
  1306.7 1.6 fusion.82
  1309.0 1.3 copy-done.1
  1310.3 3.8 copy.115
  1314.2 4.8 reshape.108
  1319.0 0.9 multiply_convert_fusion.1
  1320.5 5.8 all-to-all-start
  1326.3 1.2 copy.109
  1327.5 2.1 reshape.107
  1329.6 1.2 copy.108
  1330.7 2.0 reshape.106
  1333.0 285.1 %reduce-scatter.4.cloned.1.call-done = f32[16,512]{1,0:T(8,128)} async-done(((f32[1024,512]{1,0:T(8,128)}), f32[16,512]{1,0:T(8,128)}) %reduce-scatter.4.cloned.1.call-update) | async-done | bytes 32784
  1618.1 0.9 copy.111
  1619.0 0.7 copy.102
  (61 shorter events, 7.2 us)
Async XLA Ops:
  7.2 110.9 %all-gather.3.cloned.1.call-start = ((), (), s32[]{:S(2)}) async-start(), calls=%async_computation.3 | async-start | bytes 1064960 | tf_op jit(solution)/shard_map/all_gather | solution.py:45
  7.9 15.6 all-to-all-start.1
  16.9 691.5 %all-gather.5.cloned.1.call-start = ((), (), s32[]{:S(2)}) async-start(), calls=%async_computation.5 | async-start | bytes 1064960 | tf_op jit(solution)/shard_map/all_gather | solution.py:46
  24.3 1245.8 %all-reduce.2.cloned.1.call-start = ((), (), s32[]{:S(2)}) async-start(), calls=%async_computation.4 | async-start | bytes 4194304 | tf_op jit(solution)/shard_map/psum | solution.py:88
  699.2 4.2 copy-start.2
  708.2 909.9 %reduce-scatter.4.cloned.1.call-start = ((), (), s32[]{:S(2)}) async-start(), calls=%async_computation.6 | async-start | bytes 2129920
  1282.7 1.6 copy-start
  1285.0 1.3 copy-start.1
  1290.7 1.6 copy-start
  1293.0 1.3 copy-start.1
  1298.7 1.6 copy-start
  1301.0 1.3 copy-start.1
  1306.7 1.6 copy-start
  1309.0 1.3 copy-start.1
  1319.0 7.4 copy-start.3
  1320.5 12.5 all-to-all-start
  1327.5 2.1 copy-start.4
Sparse Core Ops, SparseCore 0:
  9.9 108.1 all-gather.2
  120.5 102.6 all-gather.4
  708.3 561.7 all-reduce.1
  1319.1 298.9 reduce-scatter.3
where the time goes:
time: 1630 us
  waiting for transfers between devices  937 us (57%)
  blocking collectives  553 us (34%)
  local copies, waits for them, and re-layouts  52 us (3%)
  matrix products  45 us (3%)
    psum x1, waiting for transfers between devices, local(): summed = lax.psum(partial_value, ('grp', 'seq'))  555 us
    unnamed x5, waiting for transfers between devices  286 us
    pmax x1, blocking collectives, local(): row_top = lax.pmax(top, ('grp', 'seq'))  278 us
    psum x1, blocking collectives, local(): row_total = lax.psum(total * jnp.exp(top - row_top), ('grp', 'seq'))  275 us
    all_gather x1, waiting for transfers between devices, local(): lax.all_gather(queries, ('grp', 'seq'), axis=0, tiled=True)  93.7 us
  transfers between devices with their start and end apart: 6, of which 5 were waited for; matrix products, arithmetic and copies ran while one was open for 3% of the time, Pallas kernels for 0%

commit v1 on v0

v1 whole, which is shorter than its diff:
```python
import jax
import jax.numpy as jnp
from jax import lax
from jax.experimental import pallas as pl
from jax.experimental.pallas import tpu as pltpu
from jax.sharding import PartitionSpec as P

MESH = pl.DeviceIdType.MESH
CHIPS = 32
PEERS = CHIPS - 1
BF = jnp.bfloat16
F32 = jnp.float32


def peer_of(me, i):
    x, z, y = me // 8, (me // 4) % 2, me % 4
    return ((x + i // 8) % 4) * 8 + ((z + (i // 4) % 2) % 2) * 4 + (y + i % 4) % 4


def stat_owner(u):
    x, k = u % 4, u // 4
    return x * 8 + (k % 2) * 4 + (k + x) % 4


def dot(a, b):
    return lax.dot_general(a, b, (((1,), (0,)), ((), ())), preferred_element_type=F32)


def dot_nt(a, b):
    return lax.dot_general(a, b, (((1,), (1,)), ((), ())), preferred_element_type=F32)


def columns(hp):
    return pl.ds(pl.multiple_of(hp * 128, 128), 128)


def kernel(
    pad_ref, q_ref, k_ref, v_ref, g_ref,
    ctx_ref, dq_ref, dk_ref, dv_ref,
    gsend, grecv, gmine, qall, gall, qt_s, gt_s, vkt, ep, oab,
    st, stsib, cst, strecv, resall, obuf, sibbuf, rsbuf, crecv,
    hsem, gat_s, gat_r, sib_s, sib_r, ss_s, ss_r, sr_s, sr_r, rs_s, rs_r, csem,
):
    core = lax.axis_index("grp")
    me = lax.axis_index("seq")
    head = lax.axis_index("head")
    other = 1 - core
    sibling = {"grp": other}

    barrier = pltpu.get_barrier_semaphore()

    @pl.loop(1, CHIPS)
    def _(i):
        pl.semaphore_signal(barrier, inc=1, device_id={"seq": peer_of(me, i)}, device_id_type=MESH)

    pl.semaphore_signal(barrier, inc=1, device_id=sibling, device_id_type=MESH)
    for j in (1, 2, 3):
        pl.semaphore_signal(barrier, inc=1, device_id={"head": (head + j) % 4}, device_id_type=MESH)

    @pl.loop(0, 8)
    def _(i):
        pair, hp = i // 4, i % 4
        kt = k_ref[pair, :, columns(hp)].T
        vt = v_ref[pair, :, columns(hp)].T
        for hh in range(2):
            vkt[pair, 2 * hp + hh, 0:64, :] = vt[64 * hh : 64 * hh + 64]
            vkt[pair, 2 * hp + hh, 64:128, :] = kt[64 * hh : 64 * hh + 64]
            vkt[pair, 2 * hp + hh, 128:144, :] = jnp.ones((16, 512), BF)

    place = (
        lax.broadcasted_iota(jnp.int32, (16, 4), 0) == lax.broadcasted_iota(jnp.int32, (16, 4), 1) + 4 * head
    ).astype(BF)
    for p in range(4):
        gsend[p] = dot(place, g_ref[:, p * 512 : (p + 1) * 512]).astype(BF)

    pl.semaphore_wait(barrier, PEERS + 4)

    def to_head(src, dst, sems, j):
        p = (head + j) % 4
        return pltpu.make_async_remote_copy(
            src(p), dst.at[head], sems.at[j], sems.at[4 + head], device_id={"head": p}, device_id_type=MESH
        )

    def from_head(src, dst, sems, j):
        p = (head + j) % 4
        return pltpu.make_async_remote_copy(
            src(p), dst.at[p], sems.at[j], sems.at[4 + p], device_id={"head": p}, device_id_type=MESH
        )

    def spread(src, dst, send, recv):
        @pl.loop(1, CHIPS)
        def _(i):
            p = peer_of(me, i)
            pltpu.make_async_remote_copy(
                src(p), dst.at[me], send, recv, device_id={"seq": p}, device_id_type=MESH
            ).start()

    def landed(dst, send, recv):
        whole = dst.at[pl.ds(0, PEERS)]
        copy = pltpu.make_async_remote_copy(
            whole, whole, send, recv, device_id=sibling, device_id_type=MESH
        )
        copy.wait_recv()
        copy.wait_send()

    def across(src, dst, k):
        return pltpu.make_async_remote_copy(
            src, dst, sib_s.at[k], sib_r.at[k], device_id=sibling, device_id_type=MESH
        )

    for j in (1, 2, 3):
        to_head(lambda p: gsend.at[p], grecv, hsem, j).start()
    spread(lambda p: q_ref, qall.at[0], gat_s.at[0], gat_r.at[0])
    qall[0, me] = q_ref[...]
    grecv[head] = gsend[head]
    for j in (1, 2, 3):
        from_head(lambda p: gsend.at[p], grecv, hsem, j).wait()

    pad_mine = pad_ref[core]
    token = lax.broadcasted_iota(jnp.int32, (16, 512), 0) + me * 16
    valid = token < 512 - pad_mine
    gsum = (grecv[0].astype(F32) + grecv[1].astype(F32)) + (grecv[2].astype(F32) + grecv[3].astype(F32))
    gown = jnp.where(valid, gsum, 0.0).astype(BF)
    gmine[...] = gown
    spread(lambda p: gmine, gall.at[0], gat_s.at[1], gat_r.at[1])
    gall[0, me] = gown

    longer = jnp.where(pad_ref[1] < pad_ref[0], 1, 0)
    mine_longer = longer == core
    third_slot = jnp.where(mine_longer, 0, 1)

    row = lax.broadcasted_iota(jnp.int32, (128, 256), 0)

    def only(t, hh):
        return jnp.where((row < 64) if hh == 0 else (row >= 64), t, jnp.zeros((), t.dtype))

    def forward(blk, pair, slot, half):
        @pl.loop(0, 4)
        def _(hp):
            q = qall[slot, half * 16 : half * 16 + 16, :, columns(hp)].reshape(256, 128)
            qt = (q * jnp.asarray(0.125, BF)).T
            qt_s[blk, hp] = qt
            k = k_ref[pair, :, columns(hp)]
            for hh in range(2):
                s = dot(k, only(qt, hh))
                m = jnp.max(s, axis=0, keepdims=True)
                p = jnp.exp(s - m).astype(BF)
                ep[blk, 2 * hp + hh, :, 256:512] = p
                ob = dot(vkt[pair, 2 * hp + hh], p)
                oab[blk, hp, hh, 0:128, :] = ob[0:128]
                st[blk, hp, 3 * hh : 3 * hh + 1, :] = m
                st[blk, hp, 3 * hh + 1 : 3 * hh + 2, :] = ob[128:129]

    def backward(blk, pair, slot, half):
        @pl.loop(0, 4)
        def _(hp):
            gt = gall[slot, half * 16 : half * 16 + 16, :, columns(hp)].reshape(256, 128).T
            gt_s[blk, hp] = gt
            v = v_ref[pair, :, columns(hp)]
            for hh in range(2):
                dp = dot(v, only(gt, hh))
                o = oab[blk, hp, hh, 0:64, :]
                r = jnp.sum(gt[64 * hh : 64 * hh + 64].astype(F32) * o, axis=0, keepdims=True)
                l = st[blk, hp, 3 * hh + 1 : 3 * hh + 2, :]
                e = (ep[blk, 2 * hp + hh, :, 256:512].astype(F32) * (dp - r / l)).astype(BF)
                ep[blk, 2 * hp + hh, :, 0:256] = e
                oab[blk, hp, hh, 128:192, :] = dot(vkt[pair, 2 * hp + hh, 64:128, :], e)
                st[blk, hp, 3 * hh + 2 : 3 * hh + 3, :] = r

    landed(qall.at[0], gat_s.at[0], gat_r.at[0])
    send_q = across(qall.at[0], qall.at[1], 0)
    send_q.start()
    forward(0, core, 0, 0)
    landed(gall.at[0], gat_s.at[1], gat_r.at[1])
    send_g = across(gall.at[0], gall.at[1], 1)
    send_g.start()
    send_q.wait()
    forward(1, other, 1, 0)
    forward(2, longer, third_slot, 1)
    send_g.wait()
    backward(1, other, 1, 0)
    backward(2, longer, third_slot, 1)
    backward(0, core, 0, 0)

    stat_a = across(st.at[1], stsib.at[pl.ds(0, 4)], 2)
    stat_b = across(st.at[2, pl.ds(2 * other, 2)], stsib.at[pl.ds(4, 2)], 3)
    stat_a.start()
    stat_b.start()
    stat_a.wait()
    stat_b.wait()

    @pl.loop(0, 6)
    def _(i):
        first = jnp.where(i < 4, 0, 2)
        hp = jnp.where(i < 4, i, 2 * core + i - 4)
        a = st[first, hp]
        b = stsib[i]
        for hh in range(2):
            ma, mb = a[3 * hh : 3 * hh + 1], b[3 * hh : 3 * hh + 1]
            m = jnp.maximum(ma, mb)
            wa, wb = jnp.exp(ma - m), jnp.exp(mb - m)
            rows = (
                m,
                wa * a[3 * hh + 1 : 3 * hh + 2] + wb * b[3 * hh + 1 : 3 * hh + 2],
                wa * a[3 * hh + 2 : 3 * hh + 3] + wb * b[3 * hh + 2 : 3 * hh + 3],
            )
            for j in range(3):
                cst[2 * i, 3 * hh + j : 3 * hh + j + 1, :] = rows[j][:, 0:128]
                cst[2 * i + 1, 3 * hh + j : 3 * hh + j + 1, :] = rows[j][:, 128:256]

    @pl.loop(0, 12)
    def _(u):
        to = stat_owner(u)

        @pl.when(to != me)
        def _():
            pltpu.make_async_remote_copy(
                cst.at[u], strecv.at[me], ss_s.at[u], ss_r, device_id={"seq": to}, device_id_type=MESH
            ).start()

        @pl.when(to == me)
        def _():
            strecv[me] = cst[u]

    xx, zz, yy = me // 8, (me // 4) % 2, me % 4
    kk = (yy - xx + 4) % 4
    is_owner = jnp.logical_and(kk < 3, zz == kk % 2)
    unit = kk * 4 + xx

    @pl.when(is_owner)
    def _():
        whole = strecv.at[pl.ds(0, PEERS)]
        pltpu.make_async_remote_copy(
            whole, whole, ss_s.at[0], ss_r, device_id=sibling, device_id_type=MESH
        ).wait_recv()
        for hh in range(2):
            m = strecv[:, 3 * hh, :]
            top = jnp.max(m, axis=0, keepdims=True)
            w = jnp.exp(m - top)
            inv = 1.0 / jnp.sum(w * strecv[:, 3 * hh + 1, :], axis=0, keepdims=True)
            delta = jnp.sum(w * strecv[:, 3 * hh + 2, :], axis=0, keepdims=True) * inv
            resall[0, unit, 3 * hh : 3 * hh + 1, :] = top
            resall[0, unit, 3 * hh + 1 : 3 * hh + 2, :] = inv
            resall[0, unit, 3 * hh + 2 : 3 * hh + 3, :] = delta

        @pl.loop(1, CHIPS)
        def _(i):
            pltpu.make_async_remote_copy(
                resall.at[0, unit], resall.at[0, unit], sr_s, sr_r.at[unit],
                device_id={"seq": peer_of(me, i)}, device_id_type=MESH,
            ).start()

    @pl.loop(0, 12)
    def _(u):
        to = stat_owner(u)

        @pl.when(to != me)
        def _():
            pltpu.make_async_remote_copy(
                cst.at[u], strecv.at[me], ss_s.at[u], ss_r, device_id={"seq": to}, device_id_type=MESH
            ).wait_send()
            pltpu.make_async_remote_copy(
                resall.at[0, u], resall.at[0, u], sr_s, sr_r.at[u], device_id={"seq": to}, device_id_type=MESH
            ).wait_recv()

    send_res = across(resall.at[0], resall.at[1], 4)
    send_res.start()
    send_res.wait()

    def weights(blk, hp, hh):
        if blk == 2:
            slot = jnp.where(hp // 2 == core, 0, 1)
            unit0 = 8 + (hp % 2) * 2
        else:
            slot, unit0 = blk, hp * 2
        ra, rb = resall[slot, unit0], resall[slot, unit0 + 1]

        def res(j):
            return jnp.concatenate([ra[3 * hh + j : 3 * hh + j + 1], rb[3 * hh + j : 3 * hh + j + 1]], axis=1)

        s = st[blk, hp]
        m, l, r = (s[3 * hh + j : 3 * hh + j + 1] for j in range(3))
        c = jnp.exp(m - res(0)) * res(1)
        return c, r / l - res(2)

    def totals(which):
        @pl.loop(0, 4)
        def _(hp):
            for blk in range(3):
                parts = []
                for hh in range(2):
                    c, gap = weights(blk, hp, hh)
                    if which == 0:
                        parts.append(c * oab[blk, hp, hh, 0:64, :])
                    else:
                        a, b = oab[blk, hp, hh, 128:192, :], oab[blk, hp, hh, 64:128, :]
                        parts.append((0.125 * c) * (a + gap * b))
                t = jnp.concatenate(parts, axis=0).T
                if blk < 2:
                    obuf[which, blk, 0:16, :, columns(hp)] = t.astype(BF).reshape(16, 16, 128)
                else:
                    own = jnp.where(mine_longer, t, 0.0).astype(BF)
                    their = jnp.where(mine_longer, 0.0, t).astype(BF)
                    obuf[which, 0, 16:32, :, columns(hp)] = own.reshape(16, 16, 128)
                    obuf[which, 1, 16:32, :, columns(hp)] = their.reshape(16, 16, 128)

    def combine(which):
        @pl.loop(0, CHIPS)
        def _(i):
            obuf[which, 0, i] = (obuf[which, 0, i].astype(F32) + sibbuf[which, i].astype(F32)).astype(BF)

    totals(0)
    send_o = across(obuf.at[0, 1], sibbuf.at[0], 5)
    send_o.start()
    totals(1)
    send_dq = across(obuf.at[1, 1], sibbuf.at[1], 6)
    send_dq.start()
    send_o.wait()
    combine(0)
    spread(lambda p: obuf.at[0, 0, p], rsbuf.at[0], rs_s.at[0], rs_r.at[0])
    rsbuf[0, me] = obuf[0, 0, me]
    send_dq.wait()
    combine(1)
    spread(lambda p: obuf.at[1, 0, p], rsbuf.at[1], rs_s.at[1], rs_r.at[1])
    rsbuf[1, me] = obuf[1, 0, me]

    @pl.loop(0, 4)
    def _(hp):
        zero64 = jnp.zeros((64, 512), BF)
        zero256 = jnp.zeros((64, 256), BF)
        outs = []
        for blk in range(3):
            acc = None
            for hh in range(2):
                c, gap = weights(blk, hp, hh)
                qh = qt_s[blk, hp, 64 * hh : 64 * hh + 64, :].astype(F32)
                gh = gt_s[blk, hp, 64 * hh : 64 * hh + 64, :].astype(F32)
                qc = c * qh
                wk = jnp.concatenate([qc.astype(BF), (gap * qc).astype(BF)], axis=1)
                wv = jnp.concatenate([zero256, (c * gh).astype(BF)], axis=1)
                rows = [wk, zero64, wv, zero64] if hh == 0 else [zero64, wk, zero64, wv]
                part = dot_nt(ep[blk, 2 * hp + hh], jnp.concatenate(rows, axis=0))
                acc = part if acc is None else acc + part
            outs.append(acc)
        mine = outs[0] + jnp.where(mine_longer, outs[2], 0.0)
        theirs = outs[1] + jnp.where(mine_longer, 0.0, outs[2])
        dk_ref[core, :, columns(hp)] = mine[:, 0:128].astype(BF)
        dv_ref[core, :, columns(hp)] = mine[:, 128:256].astype(BF)
        dk_ref[other, :, columns(hp)] = theirs[:, 0:128].astype(BF)
        dv_ref[other, :, columns(hp)] = theirs[:, 128:256].astype(BF)

    landed(rsbuf.at[0], rs_s.at[0], rs_r.at[0])
    attended = lax.fori_loop(
        0, CHIPS, lambda i, acc: acc + rsbuf[0, i].astype(F32), jnp.zeros((16, 512), F32)
    )
    crecv[head] = jnp.where(valid, attended, 0.0).astype(BF)
    for j in (1, 2, 3):
        to_head(lambda p: crecv.at[head], crecv, csem, j).start()
    landed(rsbuf.at[1], rs_s.at[1], rs_r.at[1])
    total = lax.fori_loop(
        0, CHIPS, lambda i, acc: acc + rsbuf[1, i].astype(F32), jnp.zeros((16, 512), F32)
    )
    dq_ref[...] = total.astype(BF)
    for j in (1, 2, 3):
        from_head(lambda p: crecv.at[head], crecv, csem, j).wait()
    pick = (
        lax.broadcasted_iota(jnp.int32, (4, 16), 1) == lax.broadcasted_iota(jnp.int32, (4, 16), 0) + 4 * head
    ).astype(BF)
    for p in range(4):
        ctx_ref[:, p * 512 : (p + 1) * 512] = dot(pick, crecv[p]).astype(BF)

    @pl.when(is_owner)
    def _():
        whole = strecv.at[pl.ds(0, PEERS)]
        pltpu.make_async_remote_copy(
            whole, whole, sr_s, ss_r, device_id=sibling, device_id_type=MESH
        ).wait_send()


def local(queries, keys, values, grad_out, pad_counts):
    vmem = pl.BlockSpec(memory_space=pltpu.VMEM)
    dma = pltpu.SemaphoreType.DMA
    return pl.pallas_call(
        kernel,
        out_shape=(
            jax.ShapeDtypeStruct(grad_out.shape, BF),
            jax.ShapeDtypeStruct(queries.shape, BF),
            jax.ShapeDtypeStruct(keys.shape, BF),
            jax.ShapeDtypeStruct(values.shape, BF),
        ),
        in_specs=[pl.BlockSpec(memory_space=pltpu.SMEM)] + [vmem] * 4,
        out_specs=(vmem,) * 4,
        scratch_shapes=[
            pltpu.VMEM((4, 16, 512), BF),
            pltpu.VMEM((4, 16, 512), BF),
            pltpu.VMEM((16, 512), BF),
            pltpu.VMEM((2, CHIPS, 16, 512), BF),
            pltpu.VMEM((2, CHIPS, 16, 512), BF),
            pltpu.VMEM((3, 4, 128, 256), BF),
            pltpu.VMEM((3, 4, 128, 256), BF),
            pltpu.VMEM((2, 8, 144, 512), BF),
            pltpu.VMEM((3, 8, 512, 512), BF),
            pltpu.VMEM((3, 4, 2, 192, 256), F32),
            pltpu.VMEM((3, 4, 8, 256), F32),
            pltpu.VMEM((6, 8, 256), F32),
            pltpu.VMEM((12, 8, 128), F32),
            pltpu.VMEM((CHIPS, 8, 128), F32),
            pltpu.VMEM((2, 12, 8, 128), F32),
            pltpu.VMEM((2, 2, CHIPS, 16, 512), BF),
            pltpu.VMEM((2, CHIPS, 16, 512), BF),
            pltpu.VMEM((2, CHIPS, 16, 512), BF),
            pltpu.VMEM((4, 16, 512), BF),
            dma((8,)),
            dma((2,)),
            dma((2,)),
            dma((7,)),
            dma((7,)),
            dma((12,)),
            dma(()),
            dma(()),
            dma((12,)),
            dma((2,)),
            dma((2,)),
            dma((8,)),
        ],
        compiler_params=pltpu.CompilerParams(
            collective_id=0, has_side_effects=True, vmem_limit_bytes=52 * 2**20
        ),
    )(pad_counts, queries, keys, values, grad_out)


def solution(mesh):
    return jax.shard_map(
        local,
        mesh=mesh,
        in_specs=(
            P(("grp", "seq"), "head"),
            P(None, ("grp", "seq"), "head"),
            P(None, ("grp", "seq"), "head"),
            P(("grp", "seq", "head"), None),
            P(),
        ),
        out_specs=(
            P(("grp", "seq", "head"), None),
            P(("grp", "seq"), "head"),
            P(None, ("grp", "seq"), "head"),
            P(None, ("grp", "seq"), "head"),
        ),
        check_vma=False,
    )
```

time: 1630 us -> 85.4 us (0.05)
  waiting for transfers between devices: 937 us -> 0 us
  blocking collectives: 553 us -> 0 us
  Pallas kernels: 0 us -> 78.6 us
  local copies, waits for them, and re-layouts: 52 us -> 5.87 us
  matrix products: 45 us -> 0 us
    psum x1 -> x0, waiting for transfers between devices: 555 us -> none  [local(): summed = lax.psum(partial_value, ('grp', 'seq'))]
    unnamed x5 -> x0, waiting for transfers between devices: 286 us -> none
    pmax x1 -> x0, blocking collectives: 278 us -> none  [local(): row_top = lax.pmax(top, ('grp', 'seq'))]
    psum x1 -> x0, blocking collectives: 275 us -> none  [local(): row_total = lax.psum(total * jnp.exp(top - row_top), ('grp', 'seq'))]
    all_gather x2 -> x0, waiting for transfers between devices: 93.7 us -> none  [the longest x1 93.7 us: local(): lax.all_gather(queries, ('grp', 'seq'), axis=0, tiled=True)]
    pallas_call x0 -> x1, Pallas kernels: none -> 78.6 us  [local(): pl.pallas_call(kernel, out_shape=(jax.ShapeDtypeStruct(grad_out.shape, BF...]
    dot_general x28 -> x0, matrix products: 45 us -> none  [the longest x4 15.4 us: forward_step(): jnp.einsum('bhtp,bphd->bthd', probs.astype(jnp.bfloat16), value_block, pr...]
    unnamed x21 -> x12, local copies, waits for them, and re-layouts: 25.7 us -> 5.87 us
  transfers between devices with their start and end apart: 6 -> 0, of which waited for: 5 -> 0; matrix products, arithmetic and copies ran while one was open for 3% -> 0% of each run, Pallas kernels for 0% -> 0%
where the time goes in v1:
time: 85.4 us; the launch traced here: 85.2 us
  Pallas kernels  78.6 us (92%)
  local copies, waits for them, and re-layouts  5.87 us (7%)
    pallas_call x1, Pallas kernels, local(): pl.pallas_call(kernel, out_shape=(jax.ShapeDtypeStruct(grad_out.shape, BF...  78.6 us
    unnamed x12, local copies, waits for them, and re-layouts  5.87 us

profile of v1, /device:TPU:1, one launch (start us, length us, event | category | flops | bytes accessed | tf_op | source)
XLA Modules:
  0.0 85.2 jit_solution(7588902895009256772)
XLA Ops:
  0.6 0.0 copy-start
  0.6 0.7 copy-done
  1.4 0.0 copy-start.1
  1.4 0.7 copy-done.1
  2.1 0.0 copy-start.2
  2.1 0.7 copy-done.2
  2.7 78.6 %shard_map.84 = (bf16[4,2048]{1,0:T(4,128)(2,1)S(1)}, bf16[16,512]{1,0:T(8,128)(2,1)S(1)}, bf16[2,512,512]{2,1,0:T(8,128)(2,1)S(1)}, bf16[2,512,512]{2,1,0:T(8,128)(2,1)}) custom-call(s32[2]{0:T(128)S(1)} %copy-done.2, bf16[16,512]{1,0:T(8,128)(2,1)S(1)} %copy-done, bf16[2,512,512]{2,1,0:T(8,128)(2,1)} %k_ref.1, bf16[2,512,512]{2,1,0:T(8,128)(2,1)} %v_ref.1, ...), custom_call_target="tpu_custom_call" | custom-call | tf_op jit(solution)/shard_map/pallas_call | solution.py:383
  81.4 0.6 copy.13
  82.0 0.6 copy.14
  82.6 0.0 copy-start.3
  82.6 1.0 %copy.15 = bf16[2,512,512]{2,1,0:T(8,128)(2,1)} copy(bf16[2,512,512]{2,1,0:T(8,128)(2,1)S(1)} %get-tuple-element.10) | data formatting | bytes 2097152
  83.6 0.6 copy-done.3
  84.2 1.0 %copy.16 = bf16[2,512,512]{2,1,0:T(8,128)(2,1)} copy(bf16[2,512,512]{2,1,0:T(8,128)(2,1)S(1)} %copy-done.3) | data formatting | bytes 2097152
Async XLA Ops:
  0.6 0.7 copy-start
  1.4 0.7 copy-start.1
  2.1 0.7 copy-start.2
  82.6 1.6 %copy-start.3 = (bf16[2,512,512]{2,1,0:T(8,128)(2,1)S(1)}, bf16[2,512,512]{2,1,0:T(8,128)(2,1)}, u32[]{:S(2)}) copy-start(bf16[2,512,512]{2,1,0:T(8,128)(2,1)} %get-tuple-element.11) | copy-start | bytes 3145732

commit v2 on v1

v2 whole, which is shorter than its diff:
```python
import jax
import jax.numpy as jnp
from jax import lax
from jax.experimental import pallas as pl
from jax.experimental.pallas import tpu as pltpu
from jax.sharding import PartitionSpec as P

MESH = pl.DeviceIdType.MESH
CHIPS = 32
PEERS = CHIPS - 1
BF = jnp.bfloat16
F32 = jnp.float32


def peer_of(me, i):
    x, z, y = me // 8, (me // 4) % 2, me % 4
    return ((x + i // 8) % 4) * 8 + ((z + (i // 4) % 2) % 2) * 4 + (y + i % 4) % 4


def dot(a, b):
    return lax.dot_general(a, b, (((1,), (0,)), ((), ())), preferred_element_type=F32)


def dot_nt(a, b):
    return lax.dot_general(a, b, (((1,), (1,)), ((), ())), preferred_element_type=F32)


def columns(hp):
    return pl.ds(pl.multiple_of(hp * 128, 128), 128)


def split3(x):
    a = x.astype(BF).astype(F32)
    b = (x - a).astype(BF).astype(F32)
    return a, b, (x - a - b).astype(BF).astype(F32)


def onehot(shape, rule):
    r = lax.broadcasted_iota(jnp.int32, shape, 0)
    c = lax.broadcasted_iota(jnp.int32, shape, 1)
    return rule(r, c).astype(BF)


def kernel(
    pad_ref, q_ref, k_ref, v_ref, g_ref,
    ctx_ref, dq_ref, dk_ref, dv_ref,
    gsend, grecv, gmine, qall, gall, qt_s, gt_s, vkt, ep, ob, ab,
    st, sd, obsib, absib, stsib, sdsib, cst, comb, rsbuf, wts, own, agbuf, gst, xs, xr, crecv,
    hsem, gat_s, gat_r, sib_s, sib_r, big_s, small_s, rs_r, ag_s, ag_r, csem,
):
    core = lax.axis_index("grp")
    me = lax.axis_index("seq")
    head = lax.axis_index("head")
    other = 1 - core
    sibling = {"grp": other}
    early = me < 16

    barrier = pltpu.get_barrier_semaphore()

    @pl.loop(1, CHIPS)
    def _(i):
        pl.semaphore_signal(barrier, inc=1, device_id={"seq": peer_of(me, i)}, device_id_type=MESH)

    pl.semaphore_signal(barrier, inc=1, device_id=sibling, device_id_type=MESH)
    for j in (1, 2, 3):
        pl.semaphore_signal(barrier, inc=1, device_id={"head": (head + j) % 4}, device_id_type=MESH)

    @pl.loop(0, 8)
    def _(i):
        pair, hp = i // 4, i % 4
        kt = k_ref[pair, :, columns(hp)].T
        vt = v_ref[pair, :, columns(hp)].T
        for hh in range(2):
            vkt[pair, 2 * hp + hh, 0:64, :] = vt[64 * hh : 64 * hh + 64]
            vkt[pair, 2 * hp + hh, 64:128, :] = kt[64 * hh : 64 * hh + 64]
            vkt[pair, 2 * hp + hh, 128:144, :] = jnp.ones((16, 512), BF)

    place = onehot((16, 4), lambda r, c: r == c + 4 * head)
    for p in range(4):
        gsend[p] = dot(place, g_ref[:, p * 512 : (p + 1) * 512]).astype(BF)

    pl.semaphore_wait(barrier, PEERS + 4)

    def to_head(src, dst, sems, j):
        p = (head + j) % 4
        return pltpu.make_async_remote_copy(
            src(p), dst.at[head], sems.at[j], sems.at[4 + head], device_id={"head": p}, device_id_type=MESH
        )

    def from_head(src, dst, sems, j):
        p = (head + j) % 4
        return pltpu.make_async_remote_copy(
            src(p), dst.at[p], sems.at[j], sems.at[4 + p], device_id={"head": p}, device_id_type=MESH
        )

    def pending(ref, send, recv):
        return pltpu.make_async_remote_copy(ref, ref, send, recv, device_id=sibling, device_id_type=MESH)

    def spread(src, dst, send, recv):
        @pl.loop(1, CHIPS)
        def _(i):
            pltpu.make_async_remote_copy(
                src, dst.at[me], send, recv, device_id={"seq": peer_of(me, i)}, device_id_type=MESH
            ).start()

    def landed(dst, send, recv):
        copy = pending(dst.at[pl.ds(0, PEERS)], send, recv)
        copy.wait_recv()
        copy.wait_send()

    def across(src, dst, k):
        return pltpu.make_async_remote_copy(
            src, dst, sib_s.at[k], sib_r.at[k], device_id=sibling, device_id_type=MESH
        )

    for j in (1, 2, 3):
        to_head(lambda p: gsend.at[p], grecv, hsem, j).start()
    spread(q_ref, qall.at[0], gat_s.at[0], gat_r.at[0])
    qall[0, me] = q_ref[...]
    grecv[head] = gsend[head]
    for j in (1, 2, 3):
        from_head(lambda p: gsend.at[p], grecv, hsem, j).wait()

    token = lax.broadcasted_iota(jnp.int32, (16, 512), 0) + me * 16
    gsum = (grecv[0].astype(F32) + grecv[1].astype(F32)) + (grecv[2].astype(F32) + grecv[3].astype(F32))
    gown = jnp.where(token < 512 - pad_ref[core], gsum, 0.0).astype(BF)
    gmine[...] = gown
    spread(gmine, gall.at[0], gat_s.at[1], gat_r.at[1])
    gall[0, me] = gown

    longer = jnp.where(pad_ref[1] < pad_ref[0], 1, 0)
    mine_longer = longer == core
    third_slot = jnp.where(mine_longer, 0, 1)

    row = lax.broadcasted_iota(jnp.int32, (128, 256), 0)

    def only(t, hh):
        return jnp.where((row < 64) if hh == 0 else (row >= 64), t, jnp.zeros((), t.dtype))

    def forward(blk, pair, slot, half):
        @pl.loop(0, 4)
        def _(hp):
            q = qall[slot, half * 16 : half * 16 + 16, :, columns(hp)].reshape(256, 128)
            qt = (q * jnp.asarray(0.125, BF)).T
            qt_s[blk, hp] = qt
            k = k_ref[pair, :, columns(hp)]
            for hh in range(2):
                s = dot(k, only(qt, hh))
                m = jnp.max(s, axis=0, keepdims=True)
                p = jnp.exp(s - m).astype(BF)
                ep[blk, 2 * hp + hh, :, 256:512] = p
                o = dot(vkt[pair, 2 * hp + hh], p)
                ob[blk, hp, 64 * hh : 64 * hh + 64, :] = o[0:64].astype(BF)
                ob[blk, hp, 128 + 64 * hh : 192 + 64 * hh, :] = o[64:128].astype(BF)
                st[blk, 2 * hp + hh, 0:1, :] = m
                st[blk, 2 * hp + hh, 1:2, :] = o[128:129]

    def backward(blk, pair, slot, half):
        @pl.loop(0, 4)
        def _(hp):
            gt = gall[slot, half * 16 : half * 16 + 16, :, columns(hp)].reshape(256, 128).T
            gt_s[blk, hp] = gt
            v = v_ref[pair, :, columns(hp)]
            for hh in range(2):
                dp = dot(v, only(gt, hh))
                o = ob[blk, hp, 64 * hh : 64 * hh + 64, :].astype(F32)
                r = jnp.sum(gt[64 * hh : 64 * hh + 64].astype(F32) * o, axis=0, keepdims=True)
                d = r / st[blk, 2 * hp + hh, 1:2, :]
                e = (ep[blk, 2 * hp + hh, :, 256:512].astype(F32) * (dp - d)).astype(BF)
                ep[blk, 2 * hp + hh, :, 0:256] = e
                a = dot(vkt[pair, 2 * hp + hh, 64:128, :], e)
                ab[blk, hp, 64 * hh : 64 * hh + 64, :] = a.astype(BF)
                sd[blk, 2 * hp + hh, 0:1, :] = d

    def to_owners(which, wide, narrow):
        @pl.loop(1, CHIPS)
        def _(i):
            p = peer_of(me, i)

            @pl.when(p < 16)
            def _():
                pltpu.make_async_remote_copy(
                    comb.at[which, p, :, pl.ds(0, wide)], rsbuf.at[which, me, :, pl.ds(0, wide)],
                    big_s.at[which], rs_r.at[which], device_id={"seq": p}, device_id_type=MESH,
                ).start()

            @pl.when(p >= 16)
            def _():
                pltpu.make_async_remote_copy(
                    comb.at[which, p, :, pl.ds(0, narrow)], rsbuf.at[which, me, :, pl.ds(0, narrow)],
                    small_s.at[which], rs_r.at[which], device_id={"seq": p}, device_id_type=MESH,
                ).start()

        rsbuf[which, me] = comb[which, me]

    def owners_landed(which, wide, narrow):
        @pl.when(early)
        def _():
            pending(rsbuf.at[which, pl.ds(0, 31), :, pl.ds(0, wide)], big_s.at[which], rs_r.at[which]).wait_recv()
            pending(comb.at[which, pl.ds(0, 15), :, pl.ds(0, wide)], big_s.at[which], rs_r.at[which]).wait_send()
            pending(comb.at[which, pl.ds(0, 16), :, pl.ds(0, narrow)], small_s.at[which], rs_r.at[which]).wait_send()

        @pl.when(jnp.logical_not(early))
        def _():
            pending(rsbuf.at[which, pl.ds(0, 31), :, pl.ds(0, narrow)], big_s.at[which], rs_r.at[which]).wait_recv()
            pending(comb.at[which, pl.ds(0, 16), :, pl.ds(0, wide)], big_s.at[which], rs_r.at[which]).wait_send()
            pending(comb.at[which, pl.ds(0, 15), :, pl.ds(0, narrow)], small_s.at[which], rs_r.at[which]).wait_send()

    def place_of(i):
        first = jnp.where(i < 4, 0, 2)
        hp = jnp.where(i < 4, i, 2 * core + i - 4)
        return first, hp, pl.ds(jnp.where(i < 4, 0, 16), 16), columns(jnp.where(i < 4, i, i - 4))

    def combine_forward():
        @pl.loop(0, 6)
        def _(i):
            blk, hp, chips, cols = place_of(i)
            os, bs = [], []
            for hh in range(2):
                a, b = st[blk, 2 * hp + hh], stsib[2 * i + hh]
                m = jnp.maximum(a[0:1], b[0:1])
                wa, wb = jnp.exp(a[0:1] - m), jnp.exp(b[0:1] - m)
                cst[2 * i + hh, 0:1, :] = m
                cst[2 * i + hh, 1:2, :] = wa * a[1:2] + wb * b[1:2]
                cst[2 * i + hh, 2:3, :] = wa
                cst[2 * i + hh, 3:4, :] = wb
                for out, lo in ((os, 64 * hh), (bs, 128 + 64 * hh)):
                    x = ob[blk, hp, lo : lo + 64, :].astype(F32)
                    y = obsib[i, lo : lo + 64, :].astype(F32)
                    out.append(wa * x + wb * y)
            comb[0, chips, :, cols] = jnp.concatenate(os, axis=0).T.astype(BF).reshape(16, 16, 128)
            comb[1, chips, :, cols] = jnp.concatenate(bs, axis=0).T.astype(BF).reshape(16, 16, 128)

        m8, l8 = cst[0:8, 0, :], cst[0:8, 1, :]
        pad = jnp.zeros((128 - 48, 256), F32)
        tile = jnp.concatenate([*split3(m8), *split3(l8), pad], axis=0).T.astype(BF)
        comb[0, 0:16, :, 512:640] = tile.reshape(16, 16, 128)
        none = jnp.zeros((4, 256), F32)
        m8 = jnp.concatenate([cst[8:12, 0, :], none], axis=0)
        l8 = jnp.concatenate([cst[8:12, 1, :], none], axis=0)
        tile = jnp.concatenate([*split3(m8), *split3(l8), pad], axis=0).T.astype(BF)
        comb[0, 16:32, :, 256:384] = tile.reshape(16, 16, 128)

    def combine_backward():
        @pl.loop(0, 6)
        def _(i):
            blk, hp, chips, cols = place_of(i)
            parts = []
            for hh in range(2):
                c = cst[2 * i + hh]
                l, wa, wb = c[1:2], c[2:3], c[3:4]
                da, db = sd[blk, 2 * hp + hh, 0:1, :], sdsib[2 * i + hh, 0:1, :]
                d = (wa * st[blk, 2 * hp + hh, 1:2, :] * da + wb * stsib[2 * i + hh, 1:2, :] * db) / l
                cst[2 * i + hh, 4:5, :] = d
                lo, bo = 64 * hh, 128 + 64 * hh
                xa, xb = ab[blk, hp, lo : lo + 64, :].astype(F32), ob[blk, hp, bo : bo + 64, :].astype(F32)
                ya, yb = absib[i, lo : lo + 64, :].astype(F32), obsib[i, bo : bo + 64, :].astype(F32)
                parts.append(wa * (xa + (da - d) * xb) + wb * (ya + (db - d) * yb))
            comb[2, chips, :, cols] = jnp.concatenate(parts, axis=0).T.astype(BF).reshape(16, 16, 128)

        pad = jnp.zeros((128 - 24, 256), F32)
        tile = jnp.concatenate([*split3(cst[0:8, 4, :]), pad], axis=0).T.astype(BF)
        comb[2, 0:16, :, 512:640] = tile.reshape(16, 16, 128)
        d8 = jnp.concatenate([cst[8:12, 4, :], jnp.zeros((4, 256), F32)], axis=0)
        tile = jnp.concatenate([*split3(d8), pad], axis=0).T.astype(BF)
        comb[2, 16:32, :, 256:384] = tile.reshape(16, 16, 128)

    stat_cols = pl.ds(pl.multiple_of(jnp.where(early, 512, 256), 128), 128)
    width = jnp.where(early, 512, 256)
    inside = lax.broadcasted_iota(jnp.int32, (16, 512), 1) < width

    def expand(first):
        return onehot((128, 512), lambda r, c: (r >= first) & (r < first + 24) & ((r - first) % 8 == c // 64))

    def repeat(first):
        return onehot((128, 128), lambda r, c: (r >= first) & (r < first + 24) & ((r - first) % 8 == c % 8))

    def own_attended():
        s = rsbuf[0, :, :, stat_cols].reshape(512, 128)
        m_all = dot(s, expand(0)).reshape(CHIPS, 16, 512)
        wts[...] = jnp.exp(m_all - jnp.max(m_all, axis=0, keepdims=True))
        l_sum = jnp.sum(wts[...] * dot(s, expand(24)).reshape(CHIPS, 16, 512), axis=0)
        inv = 1.0 / jnp.where(inside, l_sum, 1.0)
        att = jnp.sum(wts[...] * rsbuf[0, :, :, 0:512].astype(F32), axis=0)
        att = jnp.where(inside, att * inv, 0.0)
        third_g = gall[third_slot, me, :, pl.ds(pl.multiple_of(256 * core, 128), 256)]
        third_g = jnp.concatenate([third_g, jnp.zeros((16, 256), BF)], axis=1)
        g = jnp.where(early, gmine[...].astype(F32), third_g.astype(F32))
        prods = split3(g * att)
        same = onehot((512, 512), lambda r, c: r // 64 == c // 64)
        to8 = onehot((512, 128), lambda r, c: r // 64 == c % 8)
        delta = sum(dot(x.astype(BF), same) for x in prods)
        delta8 = sum(dot(x.astype(BF), to8) for x in prods)
        own[0] = inv
        own[1] = delta
        m8 = dot(s, repeat(0)).reshape(CHIPS, 16, 128)
        l8 = dot(s, repeat(24)).reshape(CHIPS, 16, 128)
        top8 = jnp.max(m8, axis=0)
        l8 = jnp.sum(jnp.exp(m8 - top8[None]) * l8, axis=0)
        inv8 = 1.0 / jnp.where(l8 > 0, l8, 1.0)
        lane = lax.broadcasted_iota(jnp.int32, (16, 128), 1) // 8
        tile = jnp.zeros((16, 128), F32)
        for n, term in enumerate((*split3(top8), *split3(inv8), *split3(delta8))):
            tile = jnp.where(lane == n, term, tile)
        agbuf[0, me] = tile.astype(BF)
        spread(agbuf.at[0, me], agbuf.at[0], ag_s, ag_r)
        xs[0] = att.astype(BF)

    def own_queries():
        ds = rsbuf[2, :, :, stat_cols].reshape(512, 128)
        d_all = dot(ds, expand(0)).reshape(CHIPS, 16, 512)
        a = rsbuf[2, :, :, 0:512].astype(F32)
        b = rsbuf[1, :, :, 0:512].astype(F32)
        t = jnp.sum(wts[...] * (a + (d_all - own[1][None]) * b), axis=0)
        xs[1] = jnp.where(inside, t * own[0] * 0.125, 0.0).astype(BF)

    def settle(which):
        @pl.when(jnp.logical_not(early))
        def _():
            swap = across(xs.at[which, :, pl.ds(0, 256)], xr.at[which], 8 + which)
            swap.start()
            swap.wait()
            mine, their = xs[which, :, 0:256].astype(F32), xr[which].astype(F32)
            both = jnp.concatenate(
                [jnp.where(core == 0, mine, their), jnp.where(core == 0, their, mine)], axis=1
            )
            xs[which] = jnp.where(mine_longer, both, 0.0).astype(BF)

    landed(qall.at[0], gat_s.at[0], gat_r.at[0])
    send_q = across(qall.at[0], qall.at[1], 0)
    send_q.start()
    forward(0, core, 0, 0)
    send_q.wait()
    forward(1, other, 1, 0)
    obs_1 = across(ob.at[1], obsib.at[pl.ds(0, 4)], 2)
    st_1 = across(st.at[1], stsib.at[pl.ds(0, 8)], 3)
    obs_1.start()
    st_1.start()
    landed(gall.at[0], gat_s.at[1], gat_r.at[1])
    send_g = across(gall.at[0], gall.at[1], 1)
    send_g.start()
    forward(2, longer, third_slot, 1)
    obs_2 = across(ob.at[2, pl.ds(2 * other, 2)], obsib.at[pl.ds(4, 2)], 4)
    st_2 = across(st.at[2, pl.ds(4 * other, 4)], stsib.at[pl.ds(8, 4)], 5)
    obs_2.start()
    st_2.start()
    send_g.wait()
    obs_1.wait()
    st_1.wait()
    obs_2.wait()
    st_2.wait()
    combine_forward()
    to_owners(0, 640, 384)
    to_owners(1, 512, 256)
    backward(1, other, 1, 0)
    abs_1 = across(ab.at[1], absib.at[pl.ds(0, 4)], 6)
    sd_1 = across(sd.at[1], sdsib.at[pl.ds(0, 8)], 7)
    abs_1.start()
    sd_1.start()
    backward(2, longer, third_slot, 1)
    abs_2 = across(ab.at[2, pl.ds(2 * other, 2)], absib.at[pl.ds(4, 2)], 10)
    sd_2 = across(sd.at[2, pl.ds(4 * other, 4)], sdsib.at[pl.ds(8, 4)], 11)
    abs_2.start()
    sd_2.start()
    owners_landed(0, 640, 384)
    own_attended()
    backward(0, core, 0, 0)
    abs_1.wait()
    sd_1.wait()
    abs_2.wait()
    sd_2.wait()
    combine_backward()
    to_owners(2, 640, 384)

    settle(0)
    third_valid = token < 512 - pad_ref[core]
    crecv[head] = jnp.where(third_valid, xs[0].astype(F32), 0.0).astype(BF)
    for j in (1, 2, 3):
        to_head(lambda p: crecv.at[head], crecv, csem, j).start()

    landed(agbuf.at[0], ag_s, ag_r)
    send_ag = across(agbuf.at[0], agbuf.at[1], 12)
    send_ag.start()
    send_ag.wait()

    for blk in range(3):
        if blk < 2:
            t = agbuf[blk, 0:16].reshape(256, 128).T.astype(F32)
            terms = [t[8 * n : 8 * n + 8] for n in range(9)]
        else:
            t0 = agbuf[core, 16:32].reshape(256, 128).T.astype(F32)
            t1 = agbuf[other, 16:32].reshape(256, 128).T.astype(F32)
            terms = [
                jnp.concatenate([t0[8 * n : 8 * n + 4], t1[8 * n : 8 * n + 4]], axis=0) for n in range(9)
            ]
        top, inv, delta = (terms[n] + terms[n + 1] + terms[n + 2] for n in (0, 3, 6))
        c = jnp.exp(st[blk, :, 0, :] - top) * inv
        gap = sd[blk, :, 0, :] - delta
        for h in range(8):
            gst[blk, h, 0:1, :] = c[h : h + 1]
            gst[blk, h, 1:2, :] = gap[h : h + 1]

    @pl.loop(0, 4)
    def _(hp):
        zero64 = jnp.zeros((64, 512), BF)
        zero256 = jnp.zeros((64, 256), BF)
        outs = []
        for blk in range(3):
            acc = None
            for hh in range(2):
                c, gap = gst[blk, 2 * hp + hh, 0:1, :], gst[blk, 2 * hp + hh, 1:2, :]
                qh = qt_s[blk, hp, 64 * hh : 64 * hh + 64, :].astype(F32)
                gh = gt_s[blk, hp, 64 * hh : 64 * hh + 64, :].astype(F32)
                qc = c * qh
                wk = jnp.concatenate([qc.astype(BF), (gap * qc).astype(BF)], axis=1)
                wv = jnp.concatenate([zero256, (c * gh).astype(BF)], axis=1)
                rows = [wk, zero64, wv, zero64] if hh == 0 else [zero64, wk, zero64, wv]
                part = dot_nt(ep[blk, 2 * hp + hh], jnp.concatenate(rows, axis=0))
                acc = part if acc is None else acc + part
            outs.append(acc)
        mine = outs[0] + jnp.where(mine_longer, outs[2], 0.0)
        theirs = outs[1] + jnp.where(mine_longer, 0.0, outs[2])
        dk_ref[core, :, columns(hp)] = mine[:, 0:128].astype(BF)
        dv_ref[core, :, columns(hp)] = mine[:, 128:256].astype(BF)
        dk_ref[other, :, columns(hp)] = theirs[:, 0:128].astype(BF)
        dv_ref[other, :, columns(hp)] = theirs[:, 128:256].astype(BF)

    for j in (1, 2, 3):
        from_head(lambda p: crecv.at[head], crecv, csem, j).wait()
    pick = onehot((4, 16), lambda r, c: c == r + 4 * head)
    for p in range(4):
        ctx_ref[:, p * 512 : (p + 1) * 512] = dot(pick, crecv[p]).astype(BF)

    owners_landed(1, 512, 256)
    owners_landed(2, 640, 384)
    own_queries()
    settle(1)
    dq_ref[...] = xs[1]


def local(queries, keys, values, grad_out, pad_counts):
    vmem = pl.BlockSpec(memory_space=pltpu.VMEM)
    dma = pltpu.SemaphoreType.DMA
    return pl.pallas_call(
        kernel,
        out_shape=(
            jax.ShapeDtypeStruct(grad_out.shape, BF),
            jax.ShapeDtypeStruct(queries.shape, BF),
            jax.ShapeDtypeStruct(keys.shape, BF),
            jax.ShapeDtypeStruct(values.shape, BF),
        ),
        in_specs=[pl.BlockSpec(memory_space=pltpu.SMEM)] + [vmem] * 4,
        out_specs=(vmem,) * 4,
        scratch_shapes=[
            pltpu.VMEM((4, 16, 512), BF),
            pltpu.VMEM((4, 16, 512), BF),
            pltpu.VMEM((16, 512), BF),
            pltpu.VMEM((2, CHIPS, 16, 512), BF),
            pltpu.VMEM((2, CHIPS, 16, 512), BF),
            pltpu.VMEM((3, 4, 128, 256), BF),
            pltpu.VMEM((3, 4, 128, 256), BF),
            pltpu.VMEM((2, 8, 144, 512), BF),
            pltpu.VMEM((3, 8, 512, 512), BF),
            pltpu.VMEM((3, 4, 256, 256), BF),
            pltpu.VMEM((3, 4, 128, 256), BF),
            pltpu.VMEM((3, 8, 8, 256), F32),
            pltpu.VMEM((3, 8, 8, 256), F32),
            pltpu.VMEM((6, 256, 256), BF),
            pltpu.VMEM((6, 128, 256), BF),
            pltpu.VMEM((12, 8, 256), F32),
            pltpu.VMEM((12, 8, 256), F32),
            pltpu.VMEM((12, 8, 256), F32),
            pltpu.VMEM((3, CHIPS, 16, 640), BF),
            pltpu.VMEM((3, CHIPS, 16, 640), BF),
            pltpu.VMEM((CHIPS, 16, 512), F32),
            pltpu.VMEM((2, 16, 512), F32),
            pltpu.VMEM((2, CHIPS, 16, 128), BF),
            pltpu.VMEM((3, 8, 8, 256), F32),
            pltpu.VMEM((2, 16, 512), BF),
            pltpu.VMEM((2, 16, 256), BF),
            pltpu.VMEM((4, 16, 512), BF),
            dma((8,)),
            dma((2,)),
            dma((2,)),
            dma((13,)),
            dma((13,)),
            dma((3,)),
            dma((3,)),
            dma((3,)),
            dma(()),
            dma(()),
            dma((8,)),
        ],
        compiler_params=pltpu.CompilerParams(
            collective_id=0, has_side_effects=True, vmem_limit_bytes=48 * 2**20
        ),
    )(pad_counts, queries, keys, values, grad_out)


def solution(mesh):
    return jax.shard_map(
        local,
        mesh=mesh,
        in_specs=(
            P(("grp", "seq"), "head"),
            P(None, ("grp", "seq"), "head"),
            P(None, ("grp", "seq"), "head"),
            P(("grp", "seq", "head"), None),
            P(),
        ),
        out_specs=(
            P(("grp", "seq", "head"), None),
            P(("grp", "seq"), "head"),
            P(None, ("grp", "seq"), "head"),
            P(None, ("grp", "seq"), "head"),
        ),
        check_vma=False,
    )
```

time: 85.4 us -> 78.2 us (0.916)
  Pallas kernels: 78.6 us -> 69.3 us
  local copies, waits for them, and re-layouts: 5.87 us -> 7.68 us
    pallas_call x1, Pallas kernels: 78.6 us -> 69.3 us  [local(): pl.pallas_call(kernel, out_shape=(jax.ShapeDtypeStruct(grad_out.shape, BF...]
    unnamed x12 -> x14, local copies, waits for them, and re-layouts: 5.87 us -> 7.68 us
where the time goes in v2:
time: 78.2 us; the launch traced here: 77.7 us
  Pallas kernels  69.3 us (89%)
  local copies, waits for them, and re-layouts  7.68 us (10%)
    pallas_call x1, Pallas kernels, local(): pl.pallas_call(kernel, out_shape=(jax.ShapeDtypeStruct(grad_out.shape, BF...  69.3 us
    unnamed x14, local copies, waits for them, and re-layouts  7.68 us

profile of v2, /device:TPU:1, one launch (start us, length us, event | category | flops | bytes accessed | tf_op | source)
XLA Modules:
  0.0 77.7 jit_solution(15437666784450905348)
XLA Ops:
  0.6 0.0 copy-start
  0.6 1.2 %copy-done = bf16[2,512,512]{2,1,0:T(8,128)(2,1)S(1)} copy-done((bf16[2,512,512]{2,1,0:T(8,128)(2,1)S(1)}, bf16[2,512,512]{2,1,0:T(8,128)(2,1)}, u32[]{:S(2)}) %copy-start) | copy-done | bytes 1048600
  1.9 0.0 copy-start.1
  1.9 1.2 %copy-done.1 = bf16[2,512,512]{2,1,0:T(8,128)(2,1)S(1)} copy-done((bf16[2,512,512]{2,1,0:T(8,128)(2,1)S(1)}, bf16[2,512,512]{2,1,0:T(8,128)(2,1)}, u32[]{:S(2)}) %copy-start.1) | copy-done | bytes 1048600
  3.1 0.0 copy-start.2
  3.1 0.7 copy-done.2
  3.8 0.0 copy-start.3
  3.8 0.7 copy-done.3
  4.5 0.0 copy-start.4
  4.5 0.7 copy-done.4
  5.2 69.3 %shard_map.84 = (bf16[4,2048]{1,0:T(4,128)(2,1)S(1)}, bf16[16,512]{1,0:T(8,128)(2,1)S(1)}, bf16[2,512,512]{2,1,0:T(8,128)(2,1)S(1)}, bf16[2,512,512]{2,1,0:T(8,128)(2,1)S(1)}) custom-call(s32[2]{0:T(128)S(1)} %copy-done.4, bf16[16,512]{1,0:T(8,128)(2,1)S(1)} %copy-done.2, bf16[2,512,512]{2,1,0:T(8,128)(2,1)S(1)} %copy-done, ...), custom_call_target="tpu_custom_call" | custom-call | tf_op jit(solution)/shard_map/pallas_call | solution.py:444
  74.5 0.6 copy.13
  75.1 0.6 copy.14
  75.7 1.0 %copy.15 = bf16[2,512,512]{2,1,0:T(8,128)(2,1)} copy(bf16[2,512,512]{2,1,0:T(8,128)(2,1)S(1)} %get-tuple-element.10) | data formatting | bytes 2097152
  76.7 1.0 %copy.16 = bf16[2,512,512]{2,1,0:T(8,128)(2,1)} copy(bf16[2,512,512]{2,1,0:T(8,128)(2,1)S(1)} %get-tuple-element.11) | data formatting | bytes 2097152
Async XLA Ops:
  0.6 1.2 %copy-start = (bf16[2,512,512]{2,1,0:T(8,128)(2,1)S(1)}, bf16[2,512,512]{2,1,0:T(8,128)(2,1)}, u32[]{:S(2)}) copy-start(bf16[2,512,512]{2,1,0:T(8,128)(2,1)} %k_ref.1) | copy-start | bytes 3145732
  1.9 1.2 %copy-start.1 = (bf16[2,512,512]{2,1,0:T(8,128)(2,1)S(1)}, bf16[2,512,512]{2,1,0:T(8,128)(2,1)}, u32[]{:S(2)}) copy-start(bf16[2,512,512]{2,1,0:T(8,128)(2,1)} %v_ref.1) | copy-start | bytes 3145732
  3.1 0.7 copy-start.2
  3.8 0.7 copy-start.3
  4.5 0.7 copy-start.4

commit v3 on v2

--- a/solution.py
+++ b/solution.py
@@ -42,11 +42,12 @@
 
 
 def kernel(
-    pad_ref, q_ref, k_ref, v_ref, g_ref,
+    pad_ref, q_hbm, k_hbm, v_hbm, g_hbm,
     ctx_ref, dq_ref, dk_ref, dv_ref,
+    q_ref, k_ref, v_ref, g_ref,
     gsend, grecv, gmine, qall, gall, qt_s, gt_s, vkt, ep, ob, ab,
-    st, sd, obsib, absib, stsib, sdsib, cst, comb, rsbuf, wts, own, agbuf, gst, xs, xr, crecv,
-    hsem, gat_s, gat_r, sib_s, sib_r, big_s, small_s, rs_r, ag_s, ag_r, csem,
+    st, sd, obsib, absib, stsib, sdsib, cst, oc, sbuf, comb, rsbuf, wts, own, ddev, agbuf, gst, xs, xr, crecv,
+    lsem, hsem, gat_s, gat_r, sib_s, sib_r, big_s, small_s, rs_r, ag_s, ag_r, csem,
 ):
     core = lax.axis_index("grp")
     me = lax.axis_index("seq")
@@ -64,6 +65,15 @@
     pl.semaphore_signal(barrier, inc=1, device_id=sibling, device_id_type=MESH)
     for j in (1, 2, 3):
         pl.semaphore_signal(barrier, inc=1, device_id={"head": (head + j) % 4}, device_id_type=MESH)
+
+    loads = [
+        pltpu.make_async_copy(src, dst, lsem.at[n])
+        for n, (src, dst) in enumerate(((g_hbm, g_ref), (q_hbm, q_ref), (k_hbm, k_ref), (v_hbm, v_ref)))
+    ]
+    for load in loads:
+        load.start()
+    for load in loads:
+        load.wait()
 
     @pl.loop(0, 8)
     def _(i):
@@ -137,61 +147,71 @@
     def only(t, hh):
         return jnp.where((row < 64) if hh == 0 else (row >= 64), t, jnp.zeros((), t.dtype))
 
-    def forward(blk, pair, slot, half):
-        @pl.loop(0, 4)
-        def _(hp):
-            q = qall[slot, half * 16 : half * 16 + 16, :, columns(hp)].reshape(256, 128)
-            qt = (q * jnp.asarray(0.125, BF)).T
-            qt_s[blk, hp] = qt
-            k = k_ref[pair, :, columns(hp)]
-            for hh in range(2):
-                s = dot(k, only(qt, hh))
-                m = jnp.max(s, axis=0, keepdims=True)
-                p = jnp.exp(s - m).astype(BF)
-                ep[blk, 2 * hp + hh, :, 256:512] = p
-                o = dot(vkt[pair, 2 * hp + hh], p)
-                ob[blk, hp, 64 * hh : 64 * hh + 64, :] = o[0:64].astype(BF)
-                ob[blk, hp, 128 + 64 * hh : 192 + 64 * hh, :] = o[64:128].astype(BF)
-                st[blk, 2 * hp + hh, 0:1, :] = m
-                st[blk, 2 * hp + hh, 1:2, :] = o[128:129]
-
-    def backward(blk, pair, slot, half):
-        @pl.loop(0, 4)
-        def _(hp):
-            gt = gall[slot, half * 16 : half * 16 + 16, :, columns(hp)].reshape(256, 128).T
-            gt_s[blk, hp] = gt
-            v = v_ref[pair, :, columns(hp)]
-            for hh in range(2):
-                dp = dot(v, only(gt, hh))
-                o = ob[blk, hp, 64 * hh : 64 * hh + 64, :].astype(F32)
-                r = jnp.sum(gt[64 * hh : 64 * hh + 64].astype(F32) * o, axis=0, keepdims=True)
-                d = r / st[blk, 2 * hp + hh, 1:2, :]
-                e = (ep[blk, 2 * hp + hh, :, 256:512].astype(F32) * (dp - d)).astype(BF)
-                ep[blk, 2 * hp + hh, :, 0:256] = e
-                a = dot(vkt[pair, 2 * hp + hh, 64:128, :], e)
-                ab[blk, hp, 64 * hh : 64 * hh + 64, :] = a.astype(BF)
-                sd[blk, 2 * hp + hh, 0:1, :] = d
-
-    def to_owners(which, wide, narrow):
+    def pair_of(blk):
+        return jnp.where(blk == 0, core, jnp.where(blk == 1, other, longer))
+
+    def tokens_of(buf, slot, blk, hp):
+        return buf[slot, pl.ds(16 * (blk // 2), 16), :, columns(hp)].reshape(256, 128).T
+
+    def scores(i):
+        blk, hp = i // 4, i % 4
+        qt = tokens_of(qall, blk, blk, hp) * jnp.asarray(0.125, BF)
+        qt_s[blk, hp] = qt
+        k = k_ref[pair_of(blk), :, columns(hp)]
+        for hh in range(2):
+            sbuf[i % 2, hh] = dot(k, only(qt, hh))
+
+    def forward(i):
+        blk, hp = i // 4, i % 4
+        pair = pair_of(blk)
+        now = [sbuf[i % 2, hh] for hh in range(2)]
+        scores(jnp.minimum(i + 1, 11))
+        for hh in range(2):
+            m = jnp.max(now[hh], axis=0, keepdims=True)
+            p = jnp.exp(now[hh] - m).astype(BF)
+            ep[blk, 2 * hp + hh, :, 256:512] = p
+            o = dot(vkt[pair, 2 * hp + hh], p)
+            ob[blk, hp, 64 * hh : 64 * hh + 64, :] = o[0:64].astype(BF)
+            ob[blk, hp, 128 + 64 * hh : 192 + 64 * hh, :] = o[64:128].astype(BF)
+            st[blk, 2 * hp + hh, 0:1, :] = m
+            st[blk, 2 * hp + hh, 1:2, :] = o[128:129]
+
+    def backward(i):
+        blk, hp = (i // 4 + 1) % 3, i % 4
+        pair = pair_of(blk)
+        gt = tokens_of(gall, jnp.where(blk == 2, third_slot, blk), blk, hp)
+        gt_s[blk, hp] = gt
+        v = v_ref[pair, :, columns(hp)]
+        dps = [dot(v, only(gt, hh)) for hh in range(2)]
+        for hh in range(2):
+            o = ob[blk, hp, 64 * hh : 64 * hh + 64, :].astype(F32)
+            r = jnp.sum(gt[64 * hh : 64 * hh + 64].astype(F32) * o, axis=0, keepdims=True)
+            d = r / st[blk, 2 * hp + hh, 1:2, :]
+            e = (ep[blk, 2 * hp + hh, :, 256:512].astype(F32) * (dps[hh] - d)).astype(BF)
+            ep[blk, 2 * hp + hh, :, 0:256] = e
+            a = dot(vkt[pair, 2 * hp + hh, 64:128, :], e)
+            ab[blk, hp, 64 * hh : 64 * hh + 64, :] = a.astype(BF)
+            sd[blk, 2 * hp + hh, 0:1, :] = d
+
+    def to_owners(which, wide, narrow, halves=(0, 1)):
         @pl.loop(1, CHIPS)
         def _(i):
             p = peer_of(me, i)
-
-            @pl.when(p < 16)
+            for half, cols, sems in ((0, wide, big_s), (1, narrow, small_s)):
+                if half in halves:
+
+                    @pl.when(p // 16 == half)
+                    def _():
+                        pltpu.make_async_remote_copy(
+                            comb.at[which, p, :, pl.ds(0, cols)], rsbuf.at[which, me, :, pl.ds(0, cols)],
+                            sems.at[which], rs_r.at[which], device_id={"seq": p}, device_id_type=MESH,
+                        ).start()
+
+        for half in halves:
+
+            @pl.when(me // 16 == half)
             def _():
-                pltpu.make_async_remote_copy(
-                    comb.at[which, p, :, pl.ds(0, wide)], rsbuf.at[which, me, :, pl.ds(0, wide)],
-                    big_s.at[which], rs_r.at[which], device_id={"seq": p}, device_id_type=MESH,
-                ).start()
-
-            @pl.when(p >= 16)
-            def _():
-                pltpu.make_async_remote_copy(
-                    comb.at[which, p, :, pl.ds(0, narrow)], rsbuf.at[which, me, :, pl.ds(0, narrow)],
-                    small_s.at[which], rs_r.at[which], device_id={"seq": p}, device_id_type=MESH,
-                ).start()
-
-        rsbuf[which, me] = comb[which, me]
+                rsbuf[which, me] = comb[which, me]
 
     def owners_landed(which, wide, narrow):
         @pl.when(early)
@@ -211,8 +231,8 @@
         hp = jnp.where(i < 4, i, 2 * core + i - 4)
         return first, hp, pl.ds(jnp.where(i < 4, 0, 16), 16), columns(jnp.where(i < 4, i, i - 4))
 
-    def combine_forward():
-        @pl.loop(0, 6)
+    def combine_forward(first, last):
+        @pl.loop(first, last)
         def _(i):
             blk, hp, chips, cols = place_of(i)
             os, bs = [], []
@@ -228,18 +248,22 @@
                     x = ob[blk, hp, lo : lo + 64, :].astype(F32)
                     y = obsib[i, lo : lo + 64, :].astype(F32)
                     out.append(wa * x + wb * y)
-            comb[0, chips, :, cols] = jnp.concatenate(os, axis=0).T.astype(BF).reshape(16, 16, 128)
+            oc[i] = jnp.concatenate(os, axis=0).astype(BF)
+            comb[0, chips, :, cols] = oc[i].T.reshape(16, 16, 128)
             comb[1, chips, :, cols] = jnp.concatenate(bs, axis=0).T.astype(BF).reshape(16, 16, 128)
 
-        m8, l8 = cst[0:8, 0, :], cst[0:8, 1, :]
+        if first == 0:
+            m8, l8 = cst[0:8, 0, :], cst[0:8, 1, :]
+        else:
+            none = jnp.zeros((4, 256), F32)
+            m8 = jnp.concatenate([cst[8:12, 0, :], none], axis=0)
+            l8 = jnp.concatenate([cst[8:12, 1, :], none], axis=0)
         pad = jnp.zeros((128 - 48, 256), F32)
-        tile = jnp.concatenate([*split3(m8), *split3(l8), pad], axis=0).T.astype(BF)
-        comb[0, 0:16, :, 512:640] = tile.reshape(16, 16, 128)
-        none = jnp.zeros((4, 256), F32)
-        m8 = jnp.concatenate([cst[8:12, 0, :], none], axis=0)
-        l8 = jnp.concatenate([cst[8:12, 1, :], none], axis=0)
-        tile = jnp.concatenate([*split3(m8), *split3(l8), pad], axis=0).T.astype(BF)
-        comb[0, 16:32, :, 256:384] = tile.reshape(16, 16, 128)
+        tile = jnp.concatenate([*split3(m8), *split3(l8), pad], axis=0).T.astype(BF).reshape(16, 16, 128)
+        if first == 0:
+            comb[0, 0:16, :, 512:640] = tile
+        else:
+            comb[0, 16:32, :, 256:384] = tile
 
     def combine_backward():
         @pl.loop(0, 6)
@@ -250,20 +274,13 @@
                 c = cst[2 * i + hh]
                 l, wa, wb = c[1:2], c[2:3], c[3:4]
                 da, db = sd[blk, 2 * hp + hh, 0:1, :], sdsib[2 * i + hh, 0:1, :]
-                d = (wa * st[blk, 2 * hp + hh, 1:2, :] * da + wb * stsib[2 * i + hh, 1:2, :] * db) / l
-                cst[2 * i + hh, 4:5, :] = d
                 lo, bo = 64 * hh, 128 + 64 * hh
+                gt = gt_s[blk, hp, lo : lo + 64, :].astype(F32)
+                d = jnp.sum(gt * oc[i, lo : lo + 64, :].astype(F32), axis=0, keepdims=True) / l
                 xa, xb = ab[blk, hp, lo : lo + 64, :].astype(F32), ob[blk, hp, bo : bo + 64, :].astype(F32)
                 ya, yb = absib[i, lo : lo + 64, :].astype(F32), obsib[i, bo : bo + 64, :].astype(F32)
                 parts.append(wa * (xa + (da - d) * xb) + wb * (ya + (db - d) * yb))
-            comb[2, chips, :, cols] = jnp.concatenate(parts, axis=0).T.astype(BF).reshape(16, 16, 128)
-
-        pad = jnp.zeros((128 - 24, 256), F32)
-        tile = jnp.concatenate([*split3(cst[0:8, 4, :]), pad], axis=0).T.astype(BF)
-        comb[2, 0:16, :, 512:640] = tile.reshape(16, 16, 128)
-        d8 = jnp.concatenate([cst[8:12, 4, :], jnp.zeros((4, 256), F32)], axis=0)
-        tile = jnp.concatenate([*split3(d8), pad], axis=0).T.astype(BF)
-        comb[2, 16:32, :, 256:384] = tile.reshape(16, 16, 128)
+            comb[2, chips, :, cols] = jnp.concatenate(parts, axis=0).astype(BF).T.reshape(16, 16, 128)
 
     stat_cols = pl.ds(pl.multiple_of(jnp.where(early, 512, 256), 128), 128)
     width = jnp.where(early, 512, 256)
@@ -279,20 +296,25 @@
         s = rsbuf[0, :, :, stat_cols].reshape(512, 128)
         m_all = dot(s, expand(0)).reshape(CHIPS, 16, 512)
         wts[...] = jnp.exp(m_all - jnp.max(m_all, axis=0, keepdims=True))
-        l_sum = jnp.sum(wts[...] * dot(s, expand(24)).reshape(CHIPS, 16, 512), axis=0)
+        l_all = dot(s, expand(24)).reshape(CHIPS, 16, 512)
+        l_sum = jnp.sum(wts[...] * l_all, axis=0)
         inv = 1.0 / jnp.where(inside, l_sum, 1.0)
         att = jnp.sum(wts[...] * rsbuf[0, :, :, 0:512].astype(F32), axis=0)
         att = jnp.where(inside, att * inv, 0.0)
         third_g = gall[third_slot, me, :, pl.ds(pl.multiple_of(256 * core, 128), 256)]
         third_g = jnp.concatenate([third_g, jnp.zeros((16, 256), BF)], axis=1)
         g = jnp.where(early, gmine[...].astype(F32), third_g.astype(F32))
+        dprod = jnp.where(inside[None], rsbuf[0, :, :, 0:512].astype(F32) * g[None], 0.0).reshape(512, 512)
+        high = dprod.astype(BF)
+        low = (dprod - high.astype(F32)).astype(BF)
         prods = split3(g * att)
         same = onehot((512, 512), lambda r, c: r // 64 == c // 64)
         to8 = onehot((512, 128), lambda r, c: r // 64 == c % 8)
         delta = sum(dot(x.astype(BF), same) for x in prods)
+        d_dev = (dot(high, same) + dot(low, same)).reshape(CHIPS, 16, 512)
+        ddev[...] = d_dev / jnp.where(inside[None], l_all, 1.0) - delta[None]
         delta8 = sum(dot(x.astype(BF), to8) for x in prods)
-        own[0] = inv
-        own[1] = delta
+        own[...] = inv
         m8 = dot(s, repeat(0)).reshape(CHIPS, 16, 128)
         l8 = dot(s, repeat(24)).reshape(CHIPS, 16, 128)
         top8 = jnp.max(m8, axis=0)
@@ -307,12 +329,10 @@
         xs[0] = att.astype(BF)
 
     def own_queries():
-        ds = rsbuf[2, :, :, stat_cols].reshape(512, 128)
-        d_all = dot(ds, expand(0)).reshape(CHIPS, 16, 512)
         a = rsbuf[2, :, :, 0:512].astype(F32)
         b = rsbuf[1, :, :, 0:512].astype(F32)
-        t = jnp.sum(wts[...] * (a + (d_all - own[1][None]) * b), axis=0)
-        xs[1] = jnp.where(inside, t * own[0] * 0.125, 0.0).astype(BF)
+        t = jnp.sum(wts[...] * (a + ddev[...] * b), axis=0)
+        xs[1] = jnp.where(inside, t * own[...] * 0.125, 0.0).astype(BF)
 
     def settle(which):
         @pl.when(jnp.logical_not(early))
@@ -326,51 +346,75 @@
             )
             xs[which] = jnp.where(mine_longer, both, 0.0).astype(BF)
 
-    landed(qall.at[0], gat_s.at[0], gat_r.at[0])
     send_q = across(qall.at[0], qall.at[1], 0)
-    send_q.start()
-    forward(0, core, 0, 0)
-    send_q.wait()
-    forward(1, other, 1, 0)
+    send_g = across(gall.at[0], gall.at[1], 1)
     obs_1 = across(ob.at[1], obsib.at[pl.ds(0, 4)], 2)
     st_1 = across(st.at[1], stsib.at[pl.ds(0, 8)], 3)
-    obs_1.start()
-    st_1.start()
-    landed(gall.at[0], gat_s.at[1], gat_r.at[1])
-    send_g = across(gall.at[0], gall.at[1], 1)
-    send_g.start()
-    forward(2, longer, third_slot, 1)
     obs_2 = across(ob.at[2, pl.ds(2 * other, 2)], obsib.at[pl.ds(4, 2)], 4)
     st_2 = across(st.at[2, pl.ds(4 * other, 4)], stsib.at[pl.ds(8, 4)], 5)
+    abs_1 = across(ab.at[1], absib.at[pl.ds(0, 4)], 6)
+    sd_1 = across(sd.at[1], sdsib.at[pl.ds(0, 8)], 7)
+    abs_2 = across(ab.at[2, pl.ds(2 * other, 2)], absib.at[pl.ds(4, 2)], 10)
+    sd_2 = across(sd.at[2, pl.ds(4 * other, 4)], sdsib.at[pl.ds(8, 4)], 11)
+
+    landed(qall.at[0], gat_s.at[0], gat_r.at[0])
+    send_q.start()
+    scores(0)
+
+    @pl.loop(0, 12)
+    def _(i):
+        @pl.when(i == 3)
+        def _():
+            send_q.wait()
+
+            @pl.loop(16, CHIPS)
+            def _(chip):
+                qall[2, chip] = jnp.where(mine_longer, qall[0, chip], qall[1, chip])
+
+        forward(i)
+
+        @pl.when(i == 7)
+        def _():
+            obs_1.start()
+            st_1.start()
+
     obs_2.start()
     st_2.start()
-    send_g.wait()
     obs_1.wait()
     st_1.wait()
+    combine_forward(0, 4)
+    to_owners(0, 640, 384, (0,))
     obs_2.wait()
     st_2.wait()
-    combine_forward()
-    to_owners(0, 640, 384)
-    to_owners(1, 512, 256)
-    backward(1, other, 1, 0)
-    abs_1 = across(ab.at[1], absib.at[pl.ds(0, 4)], 6)
-    sd_1 = across(sd.at[1], sdsib.at[pl.ds(0, 8)], 7)
-    abs_1.start()
-    sd_1.start()
-    backward(2, longer, third_slot, 1)
-    abs_2 = across(ab.at[2, pl.ds(2 * other, 2)], absib.at[pl.ds(4, 2)], 10)
-    sd_2 = across(sd.at[2, pl.ds(4 * other, 4)], sdsib.at[pl.ds(8, 4)], 11)
-    abs_2.start()
-    sd_2.start()
+    combine_forward(4, 6)
+    to_owners(0, 640, 384, (1,))
+    landed(gall.at[0], gat_s.at[1], gat_r.at[1])
+    send_g.start()
+    send_g.wait()
+
+    @pl.loop(0, 12)
+    def _(i):
+        backward(i)
+
+        @pl.when(i == 3)
+        def _():
+            abs_1.start()
+            sd_1.start()
+
+        @pl.when(i == 7)
+        def _():
+            abs_2.start()
+            sd_2.start()
+            to_owners(1, 512, 256)
+
     owners_landed(0, 640, 384)
     own_attended()
-    backward(0, core, 0, 0)
     abs_1.wait()
     sd_1.wait()
     abs_2.wait()
     sd_2.wait()
     combine_backward()
-    to_owners(2, 640, 384)
+    to_owners(2, 512, 256)
 
     settle(0)
     third_valid = token < 512 - pad_ref[core]
@@ -432,7 +476,7 @@
         ctx_ref[:, p * 512 : (p + 1) * 512] = dot(pick, crecv[p]).astype(BF)
 
     owners_landed(1, 512, 256)
-    owners_landed(2, 640, 384)
+    owners_landed(2, 512, 256)
     own_queries()
     settle(1)
     dq_ref[...] = xs[1]
@@ -449,13 +493,17 @@
             jax.ShapeDtypeStruct(keys.shape, BF),
             jax.ShapeDtypeStruct(values.shape, BF),
         ),
-        in_specs=[pl.BlockSpec(memory_space=pltpu.SMEM)] + [vmem] * 4,
+        in_specs=[pl.BlockSpec(memory_space=pltpu.SMEM)] + [pl.BlockSpec(memory_space=pl.ANY)] * 4,
         out_specs=(vmem,) * 4,
         scratch_shapes=[
+            pltpu.VMEM(queries.shape, BF),
+            pltpu.VMEM(keys.shape, BF),
+            pltpu.VMEM(values.shape, BF),
+            pltpu.VMEM(grad_out.shape, BF),
             pltpu.VMEM((4, 16, 512), BF),
             pltpu.VMEM((4, 16, 512), BF),
             pltpu.VMEM((16, 512), BF),
-            pltpu.VMEM((2, CHIPS, 16, 512), BF),
+            pltpu.VMEM((3, CHIPS, 16, 512), BF),
             pltpu.VMEM((2, CHIPS, 16, 512), BF),
             pltpu.VMEM((3, 4, 128, 256), BF),
             pltpu.VMEM((3, 4, 128, 256), BF),
@@ -470,15 +518,19 @@
             pltpu.VMEM((12, 8, 256), F32),
             pltpu.VMEM((12, 8, 256), F32),
             pltpu.VMEM((12, 8, 256), F32),
+            pltpu.VMEM((6, 128, 256), BF),
+            pltpu.VMEM((2, 2, 512, 256), F32),
             pltpu.VMEM((3, CHIPS, 16, 640), BF),
             pltpu.VMEM((3, CHIPS, 16, 640), BF),
             pltpu.VMEM((CHIPS, 16, 512), F32),
-            pltpu.VMEM((2, 16, 512), F32),
+            pltpu.VMEM((16, 512), F32),
+            pltpu.VMEM((CHIPS, 16, 512), F32),
             pltpu.VMEM((2, CHIPS, 16, 128), BF),
             pltpu.VMEM((3, 8, 8, 256), F32),
             pltpu.VMEM((2, 16, 512), BF),
             pltpu.VMEM((2, 16, 256), BF),
             pltpu.VMEM((4, 16, 512), BF),
+            dma((4,)),
             dma((8,)),
             dma((2,)),
             dma((2,)),

time: 78.2 us -> 65.9 us (0.84)
  Pallas kernels: 69.3 us -> 57.3 us
    pallas_call x1, Pallas kernels: 69.3 us -> 57.3 us  [local(): pl.pallas_call(kernel, out_shape=(jax.ShapeDtypeStruct(grad_out.shape, BF...]
where the time goes in v3:
time: 65.9 us; the launch traced here: 65.6 us
  Pallas kernels  57.3 us (87%)
  local copies, waits for them, and re-layouts  7.68 us (12%)
    pallas_call x1, Pallas kernels, local(): pl.pallas_call(kernel, out_shape=(jax.ShapeDtypeStruct(grad_out.shape, BF...  57.3 us
    unnamed x14, local copies, waits for them, and re-layouts  7.68 us

profile of v3, /device:TPU:1, one launch (start us, length us, event | category | flops | bytes accessed | tf_op | source)
XLA Modules:
  0.0 65.6 jit_solution(1578843648857817204)
XLA Ops:
  0.6 0.0 copy-start
  0.6 1.2 %copy-done = bf16[2,512,512]{2,1,0:T(8,128)(2,1)S(1)} copy-done((bf16[2,512,512]{2,1,0:T(8,128)(2,1)S(1)}, bf16[2,512,512]{2,1,0:T(8,128)(2,1)}, u32[]{:S(2)}) %copy-start) | copy-done | bytes 1048600
  1.9 0.0 copy-start.1
  1.9 1.2 %copy-done.1 = bf16[2,512,512]{2,1,0:T(8,128)(2,1)S(1)} copy-done((bf16[2,512,512]{2,1,0:T(8,128)(2,1)S(1)}, bf16[2,512,512]{2,1,0:T(8,128)(2,1)}, u32[]{:S(2)}) %copy-start.1) | copy-done | bytes 1048600
  3.1 0.0 copy-start.2
  3.1 0.7 %copy-done.2 = bf16[16,512]{1,0:T(8,128)(2,1)S(1)} copy-done((bf16[16,512]{1,0:T(8,128)(2,1)S(1)}, bf16[16,512]{1,0:T(8,128)(2,1)}, u32[]{:S(2)}) %copy-start.2) | copy-done | bytes 16408
  3.8 0.0 copy-start.3
  3.8 0.7 %copy-done.3 = bf16[4,2048]{1,0:T(4,128)(2,1)S(1)} copy-done((bf16[4,2048]{1,0:T(4,128)(2,1)S(1)}, bf16[4,2048]{1,0:T(4,128)(2,1)}, u32[]{:S(2)}) %copy-start.3) | copy-done | bytes 16408
  4.5 0.0 copy-start.4
  4.5 0.7 copy-done.4
  5.2 57.3 %shard_map.84 = (bf16[4,2048]{1,0:T(4,128)(2,1)S(1)}, bf16[16,512]{1,0:T(8,128)(2,1)S(1)}, bf16[2,512,512]{2,1,0:T(8,128)(2,1)S(1)}, bf16[2,512,512]{2,1,0:T(8,128)(2,1)S(1)}) custom-call(s32[2]{0:T(128)S(1)} %copy-done.4, bf16[16,512]{1,0:T(8,128)(2,1)S(1)} %copy-done.2, bf16[2,512,512]{2,1,0:T(8,128)(2,1)S(1)} %copy-done, ...), custom_call_target="tpu_custom_call" | custom-call | tf_op jit(solution)/shard_map/pallas_call | solution.py:488
  62.5 0.6 copy.13
  63.1 0.6 copy.14
  63.7 1.0 %copy.15 = bf16[2,512,512]{2,1,0:T(8,128)(2,1)} copy(bf16[2,512,512]{2,1,0:T(8,128)(2,1)S(1)} %get-tuple-element.10) | data formatting | bytes 2097152
  64.7 1.0 %copy.16 = bf16[2,512,512]{2,1,0:T(8,128)(2,1)} copy(bf16[2,512,512]{2,1,0:T(8,128)(2,1)S(1)} %get-tuple-element.11) | data formatting | bytes 2097152
Async XLA Ops:
  0.6 1.2 %copy-start = (bf16[2,512,512]{2,1,0:T(8,128)(2,1)S(1)}, bf16[2,512,512]{2,1,0:T(8,128)(2,1)}, u32[]{:S(2)}) copy-start(bf16[2,512,512]{2,1,0:T(8,128)(2,1)} %k_hbm.1) | copy-start | bytes 3145732
  1.9 1.2 %copy-start.1 = (bf16[2,512,512]{2,1,0:T(8,128)(2,1)S(1)}, bf16[2,512,512]{2,1,0:T(8,128)(2,1)}, u32[]{:S(2)}) copy-start(bf16[2,512,512]{2,1,0:T(8,128)(2,1)} %v_hbm.1) | copy-start | bytes 3145732
  3.1 0.7 %copy-start.2 = (bf16[16,512]{1,0:T(8,128)(2,1)S(1)}, bf16[16,512]{1,0:T(8,128)(2,1)}, u32[]{:S(2)}) copy-start(bf16[16,512]{1,0:T(8,128)(2,1)} %q_hbm.1) | copy-start | bytes 49156
  3.8 0.7 %copy-start.3 = (bf16[4,2048]{1,0:T(4,128)(2,1)S(1)}, bf16[4,2048]{1,0:T(4,128)(2,1)}, u32[]{:S(2)}) copy-start(bf16[4,2048]{1,0:T(4,128)(2,1)} %g_hbm.1) | copy-start | bytes 49156
  4.5 0.7 copy-start.4

commit v4 on v3

--- a/solution.py
+++ b/solution.py
@@ -13,6 +13,7 @@
 
 
 def peer_of(me, i):
+    i = 32 - i
     x, z, y = me // 8, (me // 4) % 2, me % 4
     return ((x + i // 8) % 4) * 8 + ((z + (i // 4) % 2) % 2) * 4 + (y + i % 4) % 4
 
@@ -392,7 +393,7 @@
     send_g.start()
     send_g.wait()
 
-    @pl.loop(0, 12)
+    @pl.loop(0, 12, unroll=2)
     def _(i):
         backward(i)
 
@@ -407,8 +408,11 @@
             sd_2.start()
             to_owners(1, 512, 256)
 
-    owners_landed(0, 640, 384)
-    own_attended()
+        @pl.when(i == 9)
+        def _():
+            owners_landed(0, 640, 384)
+            own_attended()
+
     abs_1.wait()
     sd_1.wait()
     abs_2.wait()
@@ -544,7 +548,7 @@
             dma((8,)),
         ],
         compiler_params=pltpu.CompilerParams(
-            collective_id=0, has_side_effects=True, vmem_limit_bytes=48 * 2**20
+            collective_id=0, has_side_effects=True, vmem_limit_bytes=50 * 2**20
         ),
     )(pad_counts, queries, keys, values, grad_out)
 

time: 65.9 us -> 63.7 us (0.967)
  local copies, waits for them, and re-layouts: 7.68 us -> 6.46 us
  Pallas kernels: 57.3 us -> 56.3 us
    unnamed x14 -> x12, local copies, waits for them, and re-layouts: 7.68 us -> 6.46 us
    pallas_call x1, Pallas kernels: 57.3 us -> 56.3 us  [local(): pl.pallas_call(kernel, out_shape=(jax.ShapeDtypeStruct(grad_out.shape, BF...]
where the time goes in v4:
time: 63.7 us; the launch traced here: 63.4 us
  Pallas kernels  56.3 us (88%)
  local copies, waits for them, and re-layouts  6.46 us (10%)
  between operations  0.65 us (1%)
    pallas_call x1, Pallas kernels, local(): pl.pallas_call(kernel, out_shape=(jax.ShapeDtypeStruct(grad_out.shape, BF...  56.3 us
    unnamed x12, local copies, waits for them, and re-layouts  6.46 us

profile of v4, /device:TPU:1, one launch (start us, length us, event | category | flops | bytes accessed | tf_op | source)
XLA Modules:
  0.0 63.4 jit_solution(1497258884118893584)
XLA Ops:
  0.6 0.0 copy-start
  0.6 1.2 %copy-done = bf16[2,512,512]{2,1,0:T(8,128)(2,1)S(1)} copy-done((bf16[2,512,512]{2,1,0:T(8,128)(2,1)S(1)}, bf16[2,512,512]{2,1,0:T(8,128)(2,1)}, u32[]{:S(2)}) %copy-start) | copy-done | bytes 1048600
  1.9 0.0 copy-start.1
  1.9 0.7 %copy-done.1 = bf16[16,512]{1,0:T(8,128)(2,1)S(1)} copy-done((bf16[16,512]{1,0:T(8,128)(2,1)S(1)}, bf16[16,512]{1,0:T(8,128)(2,1)}, u32[]{:S(2)}) %copy-start.1) | copy-done | bytes 16408
  2.6 0.0 copy-start.2
  2.6 0.7 %copy-done.2 = bf16[4,2048]{1,0:T(4,128)(2,1)S(1)} copy-done((bf16[4,2048]{1,0:T(4,128)(2,1)S(1)}, bf16[4,2048]{1,0:T(4,128)(2,1)}, u32[]{:S(2)}) %copy-start.2) | copy-done | bytes 16408
  3.3 0.0 copy-start.3
  3.3 0.7 %copy-done.3 = s32[2]{0:T(128)S(1)} copy-done((s32[2]{0:T(128)S(1)}, s32[2]{0:T(128)}, u32[]{:S(2)}) %copy-start.3) | copy-done | bytes 32
  3.9 56.3 %shard_map.84 = (bf16[4,2048]{1,0:T(4,128)(2,1)S(1)}, bf16[16,512]{1,0:T(8,128)(2,1)S(1)}, bf16[2,512,512]{2,1,0:T(8,128)(2,1)S(1)}, bf16[2,512,512]{2,1,0:T(8,128)(2,1)S(1)}) custom-call(s32[2]{0:T(128)S(1)} %copy-done.3, bf16[16,512]{1,0:T(8,128)(2,1)S(1)} %copy-done.1, bf16[2,512,512]{2,1,0:T(8,128)(2,1)S(1)} %copy-done, bf16[2,512,512]{2,1,0:T(8,128)(2,1)} %v_hbm.1, ...), custom_call_target="tpu_custom_call" | custom-call | tf_op jit(solution)/shard_map/pallas_call | solution.py:492
  60.3 0.6 copy.13
  60.9 0.6 copy.14
  61.5 1.0 %copy.15 = bf16[2,512,512]{2,1,0:T(8,128)(2,1)} copy(bf16[2,512,512]{2,1,0:T(8,128)(2,1)S(1)} %get-tuple-element.10) | data formatting | bytes 2097152
  62.5 1.0 %copy.16 = bf16[2,512,512]{2,1,0:T(8,128)(2,1)} copy(bf16[2,512,512]{2,1,0:T(8,128)(2,1)S(1)} %get-tuple-element.11) | data formatting | bytes 2097152
Async XLA Ops:
  0.6 1.2 %copy-start = (bf16[2,512,512]{2,1,0:T(8,128)(2,1)S(1)}, bf16[2,512,512]{2,1,0:T(8,128)(2,1)}, u32[]{:S(2)}) copy-start(bf16[2,512,512]{2,1,0:T(8,128)(2,1)} %k_hbm.1) | copy-start | bytes 3145732
  1.9 0.7 %copy-start.1 = (bf16[16,512]{1,0:T(8,128)(2,1)S(1)}, bf16[16,512]{1,0:T(8,128)(2,1)}, u32[]{:S(2)}) copy-start(bf16[16,512]{1,0:T(8,128)(2,1)} %q_hbm.1) | copy-start | bytes 49156
  2.6 0.7 %copy-start.2 = (bf16[4,2048]{1,0:T(4,128)(2,1)S(1)}, bf16[4,2048]{1,0:T(4,128)(2,1)}, u32[]{:S(2)}) copy-start(bf16[4,2048]{1,0:T(4,128)(2,1)} %g_hbm.1) | copy-start | bytes 49156
  3.3 0.7 %copy-start.3 = (s32[2]{0:T(128)S(1)}, s32[2]{0:T(128)}, u32[]{:S(2)}) copy-start(s32[2]{0:T(128)} %pad_ref.1) | copy-start | bytes 28

commit v5 on v4

--- a/solution.py
+++ b/solution.py
@@ -335,11 +335,12 @@
         t = jnp.sum(wts[...] * (a + ddev[...] * b), axis=0)
         xs[1] = jnp.where(inside, t * own[...] * 0.125, 0.0).astype(BF)
 
-    def settle(which):
+    def settle(which, between=lambda: None):
         @pl.when(jnp.logical_not(early))
         def _():
             swap = across(xs.at[which, :, pl.ds(0, 256)], xr.at[which], 8 + which)
             swap.start()
+            between()
             swap.wait()
             mine, their = xs[which, :, 0:256].astype(F32), xr[which].astype(F32)
             both = jnp.concatenate(
@@ -473,16 +474,18 @@
         dk_ref[other, :, columns(hp)] = theirs[:, 0:128].astype(BF)
         dv_ref[other, :, columns(hp)] = theirs[:, 128:256].astype(BF)
 
-    for j in (1, 2, 3):
-        from_head(lambda p: crecv.at[head], crecv, csem, j).wait()
-    pick = onehot((4, 16), lambda r, c: c == r + 4 * head)
-    for p in range(4):
-        ctx_ref[:, p * 512 : (p + 1) * 512] = dot(pick, crecv[p]).astype(BF)
-
+    def context():
+        for j in (1, 2, 3):
+            from_head(lambda p: crecv.at[head], crecv, csem, j).wait()
+        pick = onehot((4, 16), lambda r, c: c == r + 4 * head)
+        for p in range(4):
+            ctx_ref[:, p * 512 : (p + 1) * 512] = dot(pick, crecv[p]).astype(BF)
+
+    pl.when(early)(context)
     owners_landed(1, 512, 256)
     owners_landed(2, 512, 256)
     own_queries()
-    settle(1)
+    settle(1, context)
     dq_ref[...] = xs[1]
 
 

time: 63.7 us -> 63.6 us (level)
  no operation moved by 1% of the time
where the time goes in v5:
time: 63.6 us; the launch traced here: 63.3 us
  Pallas kernels  56.2 us (88%)
  local copies, waits for them, and re-layouts  6.46 us (10%)
  between operations  0.65 us (1%)
    pallas_call x1, Pallas kernels, local(): pl.pallas_call(kernel, out_shape=(jax.ShapeDtypeStruct(grad_out.shape, BF...  56.2 us
    unnamed x12, local copies, waits for them, and re-layouts  6.46 us

profile of v5, /device:TPU:1, one launch (start us, length us, event | category | flops | bytes accessed | tf_op | source)
XLA Modules:
  0.0 63.3 jit_solution(14848031236305874713)
XLA Ops:
  0.6 0.0 copy-start
  0.6 1.2 %copy-done = bf16[2,512,512]{2,1,0:T(8,128)(2,1)S(1)} copy-done((bf16[2,512,512]{2,1,0:T(8,128)(2,1)S(1)}, bf16[2,512,512]{2,1,0:T(8,128)(2,1)}, u32[]{:S(2)}) %copy-start) | copy-done | bytes 1048600
  1.9 0.0 copy-start.1
  1.9 0.7 %copy-done.1 = bf16[16,512]{1,0:T(8,128)(2,1)S(1)} copy-done((bf16[16,512]{1,0:T(8,128)(2,1)S(1)}, bf16[16,512]{1,0:T(8,128)(2,1)}, u32[]{:S(2)}) %copy-start.1) | copy-done | bytes 16408
  2.6 0.0 copy-start.2
  2.6 0.7 %copy-done.2 = bf16[4,2048]{1,0:T(4,128)(2,1)S(1)} copy-done((bf16[4,2048]{1,0:T(4,128)(2,1)S(1)}, bf16[4,2048]{1,0:T(4,128)(2,1)}, u32[]{:S(2)}) %copy-start.2) | copy-done | bytes 16408
  3.3 0.0 copy-start.3
  3.3 0.7 %copy-done.3 = s32[2]{0:T(128)S(1)} copy-done((s32[2]{0:T(128)S(1)}, s32[2]{0:T(128)}, u32[]{:S(2)}) %copy-start.3) | copy-done | bytes 32
  3.9 56.2 %shard_map.84 = (bf16[4,2048]{1,0:T(4,128)(2,1)S(1)}, bf16[16,512]{1,0:T(8,128)(2,1)S(1)}, bf16[2,512,512]{2,1,0:T(8,128)(2,1)S(1)}, bf16[2,512,512]{2,1,0:T(8,128)(2,1)S(1)}) custom-call(s32[2]{0:T(128)S(1)} %copy-done.3, bf16[16,512]{1,0:T(8,128)(2,1)S(1)} %copy-done.1, bf16[2,512,512]{2,1,0:T(8,128)(2,1)S(1)} %copy-done, bf16[2,512,512]{2,1,0:T(8,128)(2,1)} %v_hbm.1, ...), custom_call_target="tpu_custom_call" | custom-call | tf_op jit(solution)/shard_map/pallas_call | solution.py:495
  60.2 0.6 copy.13
  60.8 0.6 copy.14
  61.4 1.0 %copy.15 = bf16[2,512,512]{2,1,0:T(8,128)(2,1)} copy(bf16[2,512,512]{2,1,0:T(8,128)(2,1)S(1)} %get-tuple-element.10) | data formatting | bytes 2097152
  62.3 1.0 %copy.16 = bf16[2,512,512]{2,1,0:T(8,128)(2,1)} copy(bf16[2,512,512]{2,1,0:T(8,128)(2,1)S(1)} %get-tuple-element.11) | data formatting | bytes 2097152
Async XLA Ops:
  0.6 1.2 %copy-start = (bf16[2,512,512]{2,1,0:T(8,128)(2,1)S(1)}, bf16[2,512,512]{2,1,0:T(8,128)(2,1)}, u32[]{:S(2)}) copy-start(bf16[2,512,512]{2,1,0:T(8,128)(2,1)} %k_hbm.1) | copy-start | bytes 3145732
  1.9 0.7 %copy-start.1 = (bf16[16,512]{1,0:T(8,128)(2,1)S(1)}, bf16[16,512]{1,0:T(8,128)(2,1)}, u32[]{:S(2)}) copy-start(bf16[16,512]{1,0:T(8,128)(2,1)} %q_hbm.1) | copy-start | bytes 49156
  2.6 0.7 %copy-start.2 = (bf16[4,2048]{1,0:T(4,128)(2,1)S(1)}, bf16[4,2048]{1,0:T(4,128)(2,1)}, u32[]{:S(2)}) copy-start(bf16[4,2048]{1,0:T(4,128)(2,1)} %g_hbm.1) | copy-start | bytes 49156
  3.3 0.7 %copy-start.3 = (s32[2]{0:T(128)S(1)}, s32[2]{0:T(128)}, u32[]{:S(2)}) copy-start(s32[2]{0:T(128)} %pad_ref.1) | copy-start | bytes 28
